TPU v7x, 32 devices: a whole 2x2x4 slice. The times are simulated.
32 devices in a mesh: groups: 2 (over y), space: 4 (over z), test: 4 (over x, core).
Axes of the slice: x: 2, y: 2, z: 4, core: 2. Of those that a mesh axis runs over, the one named last changes fastest.
Arguments:
- log_k: bfloat16 [384, 288, 128], P(('groups', 'space')), parts along dimension 0, may hold values from -1.5 to 1.5
- heads: bfloat16 [4, 384, 288, 128], P('test', ('groups', 'space')), parts along dimension 1, may hold values from -6 to 6
- warm_adjoint: bfloat16 [4, 384, 288, 128], P('test', ('groups', 'space')), parts along dimension 1, may hold values from -6 to 6
- obs_columns: int32 [4, 128], P('test', 'groups'), parts along dimension 1, may hold values from 0 to 55295
- obs_residuals: float32 [4, 128, 128], P('test', 'groups'), parts along dimension 1, may hold values from -18 to 18
- well_columns: int32 [8], P(('groups', 'test')), parts along dimension 0, may hold values from 0 to 55295
Outputs:
- prior_gradient: float32 [384, 288, 128], P(('groups', 'space'), 'test'), parts along dimension 0
There are 2 independent parts, one for each index of `groups`. A program takes and returns all parts, laid end to end along the dimension named above; each array names one. Nothing has to cross between parts.
Inputs may be any that keep to these rules, and one draw needn't show every extreme that they name: `obs_columns`: x * 288 + y of the borehole's cell column. `well_columns`: x * 288 + y of the well's cell column.
All inputs are finite; a program needn't handle non-finite values.
Results may differ from a plain program's by a relative error of at most 0.0003.
Values may be sent and summed in bfloat16 or wider, within the bound.
A program may use at most 128 MiB of HBM per device.

v0:
```python
import jax
import jax.numpy as jnp
import numpy as np
from jax import lax
from jax.experimental import pallas as pl
from jax.experimental.pallas import tpu as pltpu
from jax.sharding import PartitionSpec as P

ITERS = 2


prior_gain = 5.0
range_squared = 4.0


def with_halo(cells, sides, width):
    for axis, dim in sides:
        count = lax.axis_size(axis)
        ends = count - 1
        head = lax.slice_in_dim(cells, 0, width, axis=dim)
        tail = lax.slice_in_dim(cells, cells.shape[dim] - width, cells.shape[dim], axis=dim)
        cells = jnp.concatenate(
            [
                lax.ppermute(tail, axis, [(i, (i + 1) % count) for i in range(ends)]),
                cells,
                lax.ppermute(head, axis, [((i + 1) % count, i) for i in range(ends)]),
            ],
            axis=dim,
        )
    return cells


def neighbours(padded):
    return [
        padded[2:, 1:-1, 1:-1],
        padded[:-2, 1:-1, 1:-1],
        padded[1:-1, 2:, 1:-1],
        padded[1:-1, :-2, 1:-1],
        padded[1:-1, 1:-1, 2:],
        padded[1:-1, 1:-1, :-2],
    ]


def operate(values, padded, conduct):
    summed = jnp.zeros_like(values)
    for face_k, beside in zip(conduct, neighbours(padded)):
        summed = summed + face_k * (values - beside)
    return summed


def kappa_of(indices, length):
    return 4.0 * jnp.sin(jnp.pi * indices / length) ** 2


def pad_sides(padded):
    return jnp.pad(padded, ((0, 0), (1, 1), (1, 1)))


def with_faces(values):
    return pad_sides(with_halo(values, (("space", 0),), 1))


def squares(residual):
    return lax.psum(jnp.sum(residual * residual), "space")


def hartley(length):
    indices = jnp.arange(length, dtype=jnp.int32)
    products = indices[:, None] * indices[None, :] % length
    angles = products.astype(jnp.float32) * (2.0 * jnp.pi / length)
    return jnp.cos(angles) + jnp.sin(angles)


def on_device(log_k, heads, warm_adjoint, obs_columns, obs_residuals, well_columns):
    slab_rows, width_cells, depth_cells = log_k.shape
    space_count = lax.axis_size("space")
    first_row = lax.axis_index("space") * slab_rows
    logk_pad, head_pad = (
        with_halo(log_k, (("space", 0),), 1),
        with_halo(heads[0], (("space", 0),), 1),
    )
    logk_val = log_k.astype(jnp.float32)
    conduct = [
        jnp.exp(0.5 * (logk_val + beside))
        for beside in neighbours(pad_sides(logk_pad.astype(jnp.float32)))
    ]
    columns = obs_columns[0]
    row_local = columns // width_cells - first_row
    inside = (row_local >= 0) & (row_local < slab_rows)
    row_local = jnp.where(inside, row_local, slab_rows)
    source = jnp.zeros((slab_rows, width_cells, depth_cells), jnp.float32)
    source = source.at[row_local, columns % width_cells].add(obs_residuals[0], mode="drop")
    adjoint = warm_adjoint[0].astype(jnp.float32)
    lam_padded = with_faces(adjoint)
    residual = source - operate(adjoint, lam_padded, conduct)
    direction = residual
    norm_now = squares(residual)
    for iteration in range(ITERS):
        dir_padded = with_faces(direction)
        applied = operate(direction, dir_padded, conduct)
        step_length = norm_now / lax.psum(jnp.sum(direction * applied), "space")
        adjoint = adjoint + step_length * direction
        lam_padded = lam_padded + step_length * dir_padded
        if iteration + 1 < ITERS:
            residual = residual - step_length * applied
            norm_next = squares(residual)
            direction = residual + norm_next / norm_now * direction
            norm_now = norm_next
    lam_full = pad_sides(with_halo(adjoint, (("space", 0),), 1))
    head_val = heads[0].astype(jnp.float32)
    misfit_term = jnp.zeros_like(adjoint)
    for face_k, lam_side, head_side in zip(
        conduct, neighbours(lam_full), neighbours(pad_sides(head_pad.astype(jnp.float32)))
    ):
        misfit_term = misfit_term + face_k * (adjoint - lam_side) * (head_val - head_side)
    column_ids = (first_row + jnp.arange(slab_rows, dtype=jnp.int32))[
        :, None
    ] * width_cells + jnp.arange(width_cells, dtype=jnp.int32)[None, :]
    keep_mask = (column_ids != well_columns[0]).astype(jnp.float32)
    partial_value = -0.5 * misfit_term * keep_mask[:, :, None]
    highest = lax.Precision.HIGHEST
    cas_depth = hartley(depth_cells)
    cas_across = hartley(width_cells)
    along_cells = slab_rows * space_count
    cas_along = hartley(along_cells)
    summed = lax.psum_scatter(partial_value, "test", scatter_dimension=1, tiled=True)
    depth_freq = jnp.einsum("xyz,zk->xky", summed, cas_depth, precision=highest)
    pencil = lax.all_to_all(depth_freq, "test", split_axis=1, concat_axis=2, tiled=True)
    across_freq = jnp.einsum("xzy,yk->kzx", pencil, cas_across, precision=highest)
    column_block = lax.all_to_all(across_freq, "space", split_axis=0, concat_axis=2, tiled=True)
    along_freq = jnp.einsum("yzx,xk->yzk", column_block, cas_along, precision=highest)
    across_rows = column_block.shape[0]
    depth_rows = column_block.shape[1]
    kappa_x = kappa_of(jnp.arange(along_cells).astype(jnp.float32), along_cells)
    kappa_y = kappa_of(
        (lax.axis_index("space") * across_rows + jnp.arange(across_rows)).astype(jnp.float32),
        width_cells,
    )
    kappa_z = kappa_of(
        (lax.axis_index("test") * depth_rows + jnp.arange(depth_rows)).astype(jnp.float32),
        depth_cells,
    )
    spectrum = (
        prior_gain
        / (
            1.0
            + range_squared
            * (kappa_y[:, None, None] + kappa_z[None, :, None] + kappa_x[None, None, :])
        )
        ** 2
    )
    along_back = jnp.einsum("yzk,kx->yzx", along_freq * spectrum, cas_along, precision=highest)
    slab_block = lax.all_to_all(along_back, "space", split_axis=2, concat_axis=0, tiled=True)
    across_back = jnp.einsum("yzx,yk->xzk", slab_block, cas_across, precision=highest)
    depth_block = lax.all_to_all(across_back, "test", split_axis=2, concat_axis=1, tiled=True)
    result = jnp.einsum("xky,kz->xyz", depth_block, cas_depth, precision=highest)
    scale_back = 1.0 / (along_cells * width_cells * depth_cells)
    return result * scale_back


def dot3(a, b):
    def split(x):
        top = x.astype(jnp.bfloat16)
        return top, (x - top.astype(jnp.float32)).astype(jnp.bfloat16)

    def dot(x, y):
        return jnp.dot(x, y, preferred_element_type=jnp.float32)

    a_top, a_low = split(a)
    b_top, b_low = split(b)
    return dot(a_top, b_top) + (dot(a_top, b_low) + dot(a_low, b_top))


VM = pl.BlockSpec(memory_space=pltpu.VMEM)
SM = pl.BlockSpec(memory_space=pltpu.SMEM)
BIG = pltpu.CompilerParams(vmem_limit_bytes=60 * 1024 * 1024)


def shape(*dims, dtype=jnp.float32):
    return jax.ShapeDtypeStruct(dims, dtype)


def iotas(plane):
    return (
        lax.broadcasted_iota(jnp.int32, plane, 0),
        lax.broadcasted_iota(jnp.int32, plane, 1),
    )


def ring_sum(plane, edge):
    rows, lanes = plane.shape
    at_row, at_lane = iotas(plane.shape)
    up = jnp.where(at_row == rows - 1, edge, pltpu.roll(plane, rows - 1, 0))
    down = jnp.where(at_row == 0, edge, pltpu.roll(plane, 1, 0))
    right = jnp.where(at_lane == lanes - 1, edge, pltpu.roll(plane, lanes - 1, 1))
    left = jnp.where(at_lane == 0, edge, pltpu.roll(plane, 1, 1))
    return (up + down) + (right + left)


def plane_total(plane):
    rows, lanes = plane.shape
    return jnp.sum(plane.reshape(rows // 8, 8, lanes), axis=0)


def swap_blocks(planes):
    count = len(planes)
    lanes = planes[0].shape[1]
    block = lanes // count
    at_lane = iotas(planes[0].shape)[1] // block
    swapped = []
    for to in range(count):
        joined = planes[to]
        for frm in range(count):
            if frm != to:
                shift = (block * (frm - to)) % lanes
                joined = jnp.where(at_lane == frm, pltpu.roll(planes[frm], shift, 1), joined)
        swapped.append(joined)
    return swapped


def residual_kernel(
    spot, columns, logk, warm, before, after, observed, start, image, soft, sums, weighted, around
):
    rows, width, depth = logk.shape
    first_row, last_row = spot[0], spot[1]

    def prepare(to, logk_row, warm_row):
        soft_row = jnp.exp(0.5 * logk_row.astype(jnp.float32))
        soft[to] = soft_row
        weighted[to] = soft_row * warm_row.astype(jnp.float32)

    for i in range(3):
        prepare(i, before[i], before[3 + i])
        prepare(rows + 3 + i, after[i], after[3 + i])

    def fill(i, _):
        prepare(i + 3, logk[i], warm[i])
        return 0

    lax.fori_loop(0, rows, fill, 0)

    def first(i, _):
        row = first_row + i - 2
        inside = ((row >= 0) & (row < last_row)).astype(jnp.float32)
        soft_row = soft[i + 1]
        near = ring_sum(soft_row, 1.0) + (soft[i] + soft[i + 2])
        around[i] = near
        held = weighted[i + 1]
        beside = ring_sum(held, 0.0) + (weighted[i] + weighted[i + 2])
        start[i] = (soft_row * beside - held * near) * inside
        return 0

    lax.fori_loop(0, rows + 4, first, 0)

    def add(o, _):
        column = columns[0, o]
        row = column // width
        place = column - row * width
        local = row - first_row + 2

        @pl.when((local >= 0) & (local < rows + 4))
        def _():
            start[local, pl.ds(place, 1), :] += observed[pl.ds(o, 1), :]

        return 0

    lax.fori_loop(0, columns.shape[1], add, 0)

    def scale(i, _):
        weighted[i] = soft[i + 1] * start[i]
        return 0

    lax.fori_loop(0, rows + 4, scale, 0)

    def second(i, carry):
        total_rr, total_rq = carry
        row = first_row + i - 1
        inside = ((row >= 0) & (row < last_row)).astype(jnp.float32)
        held = weighted[i + 1]
        beside = ring_sum(held, 0.0) + (weighted[i] + weighted[i + 2])
        applied = (held * around[i + 1] - soft[i + 2] * beside) * inside
        image[i] = applied
        value = start[i + 1]
        own = ((i >= 1) & (i <= rows)).astype(jnp.float32)
        return (
            total_rr + own * plane_total(value * value),
            total_rq + own * plane_total(value * applied),
        )

    zero = jnp.zeros((8, depth), jnp.float32)
    total_rr, total_rq = lax.fori_loop(0, rows + 2, second, (zero, zero))
    sums[0] = total_rr
    sums[1] = total_rq


def face_terms(soft, field, head, axis):
    size = soft.shape[axis]
    at = iotas(soft.shape)[axis]
    both = field * head
    ahead = size - 1
    product = (field - pltpu.roll(field, ahead, axis)) * (head - pltpu.roll(head, ahead, axis))
    upper = jnp.where(at == size - 1, both, pltpu.roll(soft, ahead, axis) * product)
    lower = jnp.where(at == 0, both, pltpu.roll(soft * product, 1, axis))
    return upper + lower


MESH = pl.DeviceIdType.MESH


def greet(others):
    barrier = pltpu.get_barrier_semaphore()
    for other in others:
        pl.semaphore_signal(barrier, inc=1, device_id=other, device_id_type=MESH)
    pl.semaphore_wait(barrier, len(others))


def gradient_kernel(
    spot,
    sums,
    warm,
    heads,
    before,
    after,
    start,
    image,
    soft,
    cas,
    out,
    field,
    head,
    mine,
    from_mate,
    from_across,
    send_mate,
    take_mate,
    send_across,
    take_across,
    shared,
    send_sum,
    take_sum,
):
    rows, width, depth = warm.shape
    slabs = shared.shape[1]
    slab = lax.axis_index("space")
    others = [{"space": lax.rem(slab + k, slabs)} for k in range(1, slabs)]
    here = lax.axis_index("test")
    half, core = here // 2, lax.rem(here, 2)
    mate = {"test": 2 * half + 1 - core}
    across = {"test": 2 * (1 - half) + core}
    greet(others + [mate, across])
    first_row = spot[0]
    well = spot[2]

    def share(turn):
        return [
            pltpu.make_async_remote_copy(
                src_ref=shared.at[turn, slab],
                dst_ref=shared.at[turn, slab],
                send_sem=send_sum.at[turn, k],
                recv_sem=take_sum.at[turn, k],
                device_id=other,
                device_id_type=MESH,
            )
            for k, other in enumerate(others)
        ]

    def gathered_sum(turn, n):
        total = shared[turn, 0, n]
        for m in range(1, slabs):
            total = total + shared[turn, m, n]
        return jnp.broadcast_to(jnp.sum(total, axis=(0, 1), keepdims=True), (1, depth))

    shared[0, slab] = sums[...]
    for copy in share(0):
        copy.start()
    head[0] = before[6]
    head[rows + 1] = after[6]

    def keep_head(i, _):
        head[i + 1] = heads[i]
        return 0

    lax.fori_loop(0, rows, keep_head, 0)
    for copy in share(0):
        copy.wait()
    norm, curve = gathered_sum(0, 0), gathered_sum(0, 1)
    length = norm / curve

    def scale(i, _):
        field[i] = soft[i + 2] * (start[i + 1] - length * image[i])
        return 0

    lax.fori_loop(0, rows + 2, scale, 0)

    def apply(i, carry):
        total_rr, total_rq = carry
        held = field[i + 1]
        beside = ring_sum(held, 0.0) + (field[i] + field[i + 2])
        near = ring_sum(soft[i + 3], 1.0) + (soft[i + 2] + soft[i + 4])
        value = start[i + 2] - length * image[i + 1]
        applied = held * near - soft[i + 3] * beside
        return total_rr + plane_total(value * value), total_rq + plane_total(value * applied)

    zero = jnp.zeros((8, depth), jnp.float32)
    total_rr, total_rq = lax.fori_loop(0, rows, apply, (zero, zero))
    shared[1, slab, 0] = total_rr
    shared[1, slab, 1] = total_rq
    for copy in share(1):
        copy.start()
    for copy in share(1):
        copy.wait()
    norm_next, curve_next = gathered_sum(1, 0), gathered_sum(1, 1)
    ratio = norm_next / norm
    length_next = norm_next / (curve_next - ratio * norm_next / length)
    with_start = length + length_next * (1.0 + ratio)
    with_image = length_next * length

    def fill(to, warm_row):
        field[to] = (
            warm_row.astype(jnp.float32) + with_start * start[to + 1] - with_image * image[to]
        )

    fill(0, before[5])
    fill(rows + 1, after[3])

    def middle(i, _):
        fill(i + 1, warm[i])
        return 0

    lax.fori_loop(0, rows, middle, 0)
    at_row = iotas((width, depth))[0]
    count = 4
    groups = rows // count

    def term(i):
        s, f, h = soft[i + 3], field[i + 1], head[i + 1].astype(jnp.float32)
        gathered = face_terms(s, f, h, 0) + face_terms(s, f, h, 1)
        gathered += soft[i + 2] * ((f - field[i]) * (h - head[i].astype(jnp.float32)))
        gathered += soft[i + 4] * ((f - field[i + 2]) * (h - head[i + 2].astype(jnp.float32)))
        keep = at_row != well - (first_row + i) * width
        value = jnp.where(keep, -0.5 * s * gathered, 0.0)
        return dot3(value, cas[...])

    def to_mate(g):
        return pltpu.make_async_remote_copy(
            src_ref=mine.at[1 - core, g],
            dst_ref=from_mate.at[g],
            send_sem=send_mate.at[g],
            recv_sem=take_mate.at[g],
            device_id=mate,
            device_id_type=MESH,
        )

    def to_across(g):
        return pltpu.make_async_remote_copy(
            src_ref=mine.at[core, g, 1 - half],
            dst_ref=from_across.at[g],
            send_sem=send_across.at[g],
            recv_sem=take_across.at[g],
            device_id=across,
            device_id_type=MESH,
        )

    def group(g):
        for t, plane in enumerate(swap_blocks([term(g * count + p) for p in range(count)])):
            mine[t % 2, g, t // 2] = plane
        to_mate(g).start()

    def relay(g):
        to_mate(g).wait_recv()
        mine[core, g, 1 - half] += from_mate[g, 1 - half]
        to_across(g).start()

    group(0)

    def step(g, _):
        group(g)
        relay(g - 1)
        return 0

    lax.fori_loop(1, groups, step, 0)
    relay(groups - 1)

    def finish(g, _):
        to_across(g).wait_recv()
        out[g] = (mine[core, g, half] + from_mate[g, half]) + from_across[g]
        to_mate(g).wait_send()
        to_across(g).wait_send()
        return 0

    lax.fori_loop(0, groups, finish, 0)


def spectral_kernel(
    summed,
    tables,
    cas_across,
    cas_depth,
    out,
    freq,
    moments,
    filtered,
    going,
    coming,
    send_end,
    take_end,
    send_back,
    take_back,
):
    groups, width, lanes = summed.shape
    count, part = going.shape[0], going.shape[2]
    rows = groups * count
    slabs = moments.shape[0]
    slab, here = lax.axis_index("space"), lax.axis_index("test")
    others = [{"space": lax.rem(slab + k, slabs)} for k in range(1, slabs)]
    peers = [lax.rem(here + k, count) for k in range(1, count)]
    greet(others + [{"test": peer} for peer in peers])

    def mix(g, _):
        mixed = dot3(cas_across[...], summed[g])
        blocks = [mixed[j * part : (j + 1) * part] for j in range(count)]
        for p, plane in enumerate(swap_blocks(blocks)):
            freq[g * count + p] = plane
        return 0

    lax.fori_loop(0, groups, mix, 0)
    pole, level, slope, decay, wrap_one, wrap_two = (tables[n] for n in range(6))

    def walk(i, carry):
        one, two, back_one, back_two = carry
        value, back = freq[i], freq[rows - 1 - i]
        return (
            value + pole * one,
            pole * (two + one),
            back + pole * back_one,
            pole * (back_two + back_one),
        )

    zero = jnp.zeros((part, lanes), jnp.float32)
    ends = lax.fori_loop(0, rows, walk, (zero, zero, zero, zero))
    for n in range(4):
        moments[slab, n] = ends[n]
    copies = [
        pltpu.make_async_remote_copy(
            src_ref=moments.at[slab],
            dst_ref=moments.at[slab],
            send_sem=send_end.at[k],
            recv_sem=take_end.at[k],
            device_id=other,
            device_id_type=MESH,
        )
        for k, other in enumerate(others)
    ]
    for copy in copies:
        copy.start()
    for copy in copies:
        copy.wait()

    def carried(direction, n):
        one, two = zero, zero
        for m in range(slabs, 0, -1):
            other = lax.rem(slab + 2 * slabs - direction * m, slabs)
            one, two = (
                decay * one + moments[other, n],
                decay * (two + rows * one) + moments[other, n + 1],
            )
        return wrap_one * one, wrap_one * two + wrap_two * one

    def forward(i, carry):
        one, two = carry
        two = pole * (two + one)
        one = freq[i] + pole * one
        filtered[i] = level * one + slope * two
        return one, two

    lax.fori_loop(0, rows, forward, carried(1, 0))

    def backward(i, carry):
        one, two = carry
        at = rows - 1 - i
        two = pole * (two + one)
        one = pole * one
        filtered[at] += level * one + slope * two
        return one + freq[at], two

    lax.fori_loop(0, rows, backward, carried(-1, 2))

    def to_peer(k, g):
        return pltpu.make_async_remote_copy(
            src_ref=going.at[peers[k], g],
            dst_ref=coming.at[here, g],
            send_sem=send_back.at[k, g],
            recv_sem=take_back.at[k, g],
            device_id={"test": peers[k]},
            device_id_type=MESH,
        )

    def unmix(g, _):
        blocks = swap_blocks([filtered[g * count + p] for p in range(count)])
        stacked = jnp.concatenate(blocks, axis=0)
        mixed = dot3(cas_across[...], stacked)
        for u in range(count):
            going[u, g] = mixed[u * part : (u + 1) * part]
        for k in range(count - 1):
            to_peer(k, g).start()
        coming[here, g] = going[here, g]
        return 0

    lax.fori_loop(0, groups, unmix, 0)

    def back(g, _):
        for k in range(count - 1):
            to_peer(k, g).wait()
        for p, plane in enumerate(swap_blocks([coming[t, g] for t in range(count)])):
            out[g * count + p] = dot3(plane, cas_depth[...])
        return 0

    lax.fori_loop(0, groups, back, 0)


def table(length):
    indices = np.arange(length)
    angles = (indices[:, None] * indices[None, :] % length) * (2.0 * np.pi / length)
    return jnp.asarray((np.cos(angles) + np.sin(angles)).astype(np.float32))


def fast(log_k, heads, warm_adjoint, obs_columns, obs_residuals, well_columns):
    rows, width, depth = log_k.shape
    slabs = lax.axis_size("space")
    count = lax.axis_size("test")
    along = rows * slabs
    part = width // count
    block = depth // count
    first_row = lax.axis_index("space") * rows
    warm, head = warm_adjoint[0], heads[0]
    low = jnp.concatenate([log_k[:3], warm[:3], head[:1]])
    high = jnp.concatenate([log_k[rows - 3 :], warm[rows - 3 :], head[rows - 1 :]])
    before = lax.ppermute(high, "space", [(i, i + 1) for i in range(slabs - 1)])
    after = lax.ppermute(low, "space", [(i + 1, i) for i in range(slabs - 1)])
    spot = jnp.stack([first_row, jnp.int32(along), well_columns[0]]).astype(jnp.int32)
    start, image, soft, sums = pl.pallas_call(
        residual_kernel,
        out_shape=[
            shape(rows + 4, width, depth),
            shape(rows + 2, width, depth),
            shape(rows + 6, width, depth),
            shape(2, 8, depth),
        ],
        in_specs=[SM, SM, VM, VM, VM, VM, VM],
        out_specs=[VM] * 4,
        scratch_shapes=[
            pltpu.VMEM((rows + 6, width, depth), jnp.float32),
            pltpu.VMEM((rows + 4, width, depth), jnp.float32),
        ],
        compiler_params=BIG,
        name="residual",
    )(spot, obs_columns, log_k, warm, before, after, obs_residuals[0])
    cas_depth = table(depth)
    cas_across = table(width)
    groups = rows // count
    summed = pl.pallas_call(
        gradient_kernel,
        out_shape=shape(groups, width, depth),
        in_specs=[SM] + [VM] * 9,
        out_specs=VM,
        scratch_shapes=[
            pltpu.VMEM((rows + 2, width, depth), jnp.float32),
            pltpu.VMEM((rows + 2, width, depth), jnp.bfloat16),
            pltpu.VMEM((2, groups, 2, width, depth), jnp.float32),
            pltpu.VMEM((groups, 2, width, depth), jnp.float32),
            pltpu.VMEM((groups, width, depth), jnp.float32),
        ]
        + [pltpu.SemaphoreType.DMA((groups,))] * 4
        + [pltpu.VMEM((2, slabs, 2, 8, depth), jnp.float32)]
        + [pltpu.SemaphoreType.DMA((2, slabs - 1))] * 2,
        compiler_params=pltpu.CompilerParams(
            vmem_limit_bytes=60 * 1024 * 1024, collective_id=1, has_side_effects=True
        ),
        name="gradient",
    )(spot, sums, warm, head, before, after, start, image, soft, cas_depth)
    lanes_at = jnp.arange(depth)
    across_at = (lanes_at // block)[None, :] * part + jnp.arange(part)[:, None]
    depth_at = lax.axis_index("test") * block + lanes_at % block
    shift = 1.0 + range_squared * (
        kappa_of(across_at.astype(jnp.float32), width)
        + kappa_of(depth_at.astype(jnp.float32), depth)[None, :]
    )
    centre = 1.0 + shift / (2.0 * range_squared)
    pole = 1.0 / (centre + jnp.sqrt(centre * centre - 1.0))
    square = pole * pole
    gain = prior_gain / (range_squared * range_squared) * square / (width * depth)
    slope = gain / (1.0 - square) ** 2
    level = slope * (1.0 + square) / (1.0 - square)
    turn = pole**along
    wrap_one = 1.0 / (1.0 - turn)
    tables = jnp.stack(
        [pole, level, slope, pole**rows, wrap_one, along * turn * wrap_one * wrap_one]
    )
    return pl.pallas_call(
        spectral_kernel,
        out_shape=shape(rows, part, depth),
        in_specs=[VM] * 4,
        out_specs=VM,
        scratch_shapes=[
            pltpu.VMEM((rows, part, depth), jnp.float32),
            pltpu.VMEM((slabs, 4, part, depth), jnp.float32),
            pltpu.VMEM((rows, part, depth), jnp.float32),
            pltpu.VMEM((count, groups, part, depth), jnp.float32),
            pltpu.VMEM((count, groups, part, depth), jnp.float32),
            pltpu.SemaphoreType.DMA((slabs - 1,)),
            pltpu.SemaphoreType.DMA((slabs - 1,)),
            pltpu.SemaphoreType.DMA((count - 1, groups)),
            pltpu.SemaphoreType.DMA((count - 1, groups)),
        ],
        compiler_params=pltpu.CompilerParams(
            vmem_limit_bytes=40 * 1024 * 1024, collective_id=2, has_side_effects=True
        ),
        name="spectral",
    )(summed, tables, cas_across, cas_depth)


def pick(log_k, *rest):
    rows, width, depth = log_k.shape
    count = lax.axis_size("test")
    fits = depth == 128 and count == 4 and rows % count == 0 and width % (8 * count) == 0
    return (fast if fits and lax.axis_size("space") > 1 else on_device)(log_k, *rest)


def solution(mesh):
    placed = (
        P(("groups", "space"), None, None),
        P("test", ("groups", "space"), None, None),
        P("test", ("groups", "space"), None, None),
        P("test", "groups"),
        P("test", "groups", None),
        P(("groups", "test")),
    )
    return jax.shard_map(
        pick,
        mesh=mesh,
        in_specs=placed,
        out_specs=P(("groups", "space"), "test", None),
        check_vma=False,
    )
```

profile of v0, /device:TPU:0, one launch (start us, length us, event | category | flops | bytes accessed | tf_op | source)
XLA Modules:
  0.0 183.2 jit_solution(14901816660691796542)
XLA Ops:
  0.0 1.1 fusion.12
  1.1 1.1 slice_bitcast_fusion
  2.2 0.9 slice_bitcast_fusion.2
  3.1 0.1 pad_maximum_fusion
  3.2 5.0 %collective-permute-start = (bf16[7,288,128]{2,1,0:T(8,128)(2,1)S(1)}, bf16[7,288,128]{2,1,0:T(8,128)(2,1)S(1)}, u32[]{:S(2)}, u32[]{:S(2)}) collective-permute-start(bf16[7,288,128]{2,1,0:T(8,128)(2,1)S(1)} %pad_maximum_fusion), channel_id=1, source_target_pairs={{0,4},{4,8},{8,12},{1,5},{5,9},{9,13},{2,6},{6,10},{10,14},{3,7},{... | collective-permute-start | bytes 1548296 | tf_op jit(solution)/shard_map/ppermute | solution.py:638
  8.1 0.1 pad_maximum_fusion.1
  8.2 1.3 collective-permute-start.1
  10.2 0.2 fusion.4
  10.4 0.2 divide_dynamic-update-slice_fusion
  10.6 0.2 fusion.3
  10.8 0.2 fusion
  11.0 0.7 pad_add_fusion.spot
  11.7 0.2 fusion.2
  11.9 0.2 fusion.1.tables
  12.1 7.0 %collective-permute-done.before = bf16[7,288,128]{2,1,0:T(8,128)(2,1)S(1)} collective-permute-done((bf16[7,288,128]{2,1,0:T(8,128)(2,1)S(1)}, bf16[7,288,128]{2,1,0:T(8,128)(2,1)S(1)}, u32[]{:S(2)}, u32[]{:S(2)}) %collective-permute-start) | collective-permute-done | bytes 516128 | tf_op jit(solution)/shard_map/ppermute | solution.py:638
  19.1 0.0 copy-start.3
  19.1 4.2 %collective-permute-done.1.after = bf16[7,288,128]{2,1,0:T(8,128)(2,1)S(1)} collective-permute-done((bf16[7,288,128]{2,1,0:T(8,128)(2,1)S(1)}, bf16[7,288,128]{2,1,0:T(8,128)(2,1)S(1)}, u32[]{:S(2)}, u32[]{:S(2)}) %collective-permute-start.1) | collective-permute-done | bytes 516128 | tf_op jit(solution)/shard_map/ppermute | solution.py:639
  23.3 0.0 copy-start.4
  23.3 0.0 copy-done.3
  23.3 0.8 copy-done.4
  24.2 34.9 %residual.1 = (f32[52,288,128]{2,1,0:T(8,128)}, f32[50,288,128]{2,1,0:T(8,128)}, f32[54,288,128]{2,1,0:T(8,128)}, f32[2,8,128]{2,1,0:T(8,128)}) custom-call(s32[3]{0:T(128)} %pad_add_fusion.spot, s32[1,64]{1,0:T(1,128)} %columns.1, bf16[48,288,128]{2,1,0:T(8,128)(2,1)} %logk.1, bf16[48,288,128]{2,1,0:T(8,128)(2,1)} %bitcast.12, ...), custom_call_target="tpu_custom_call" | custom-call | tf_op jit(solution)/shard_map/residual/pallas_call | solution.py:641
  59.1 0.0 copy-start.1
  59.1 0.0 copy-start.2
  59.1 80.0 %gradient.1.summed = f32[12,288,128]{2,1,0:T(8,128)} custom-call(s32[3]{0:T(128)} %pad_add_fusion.spot, f32[2,8,128]{2,1,0:T(8,128)} %get-tuple-element.9.sums, bf16[48,288,128]{2,1,0:T(8,128)(2,1)} %bitcast.13, bf16[48,288,128]{2,1,0:T(8,128)(2,1)} %bitcast.14, bf16[7,288,128]{2,1,0:T(8,128)(2,1)} %copy-done.3, bf16[7,288,128]{2,1,0:T(8,128)(2,1)} %copy-done.4, ...), custom_call_target="tpu_custom_call" | custom-call | tf_op jit(solution)/shard_map/gradient/pallas_call | solution.py:661
  139.1 0.0 copy-done.1
  139.2 0.0 copy-done.2
  139.2 0.0 copy-start
  139.2 1.5 copy-done
  140.6 41.3 %spectral.1 = f32[48,72,128]{2,1,0:T(8,128)S(1)} custom-call(f32[12,288,128]{2,1,0:T(8,128)S(1)} %copy-done, f32[6,72,128]{2,1,0:T(8,128)S(1)} %fusion.1.tables, f32[288,288]{1,0:T(8,128)S(1)} %copy-done.1, f32[128,128]{1,0:T(8,128)S(1)} %copy-done.2), custom_call_target="tpu_custom_call" | custom-call | tf_op jit(solution)/shard_map/spectral/pallas_call | solution.py:699
  182.0 1.2 copy.16
  (2 shorter events, 0.1 us)
Async XLA Ops:
  3.2 15.9 %collective-permute-start = (bf16[7,288,128]{2,1,0:T(8,128)(2,1)S(1)}, bf16[7,288,128]{2,1,0:T(8,128)(2,1)S(1)}, u32[]{:S(2)}, u32[]{:S(2)}) collective-permute-start(bf16[7,288,128]{2,1,0:T(8,128)(2,1)S(1)} %pad_maximum_fusion), channel_id=1, source_target_pairs={{0,4},{4,8},{8,12},{1,5},{5,9},{9,13},{2,6},{6,10},{10,14},{3,7},{... | collective-permute-start | bytes 1548296 | tf_op jit(solution)/shard_map/ppermute | solution.py:638
  8.2 15.1 %collective-permute-start.1 = (bf16[7,288,128]{2,1,0:T(8,128)(2,1)S(1)}, bf16[7,288,128]{2,1,0:T(8,128)(2,1)S(1)}, u32[]{:S(2)}, u32[]{:S(2)}) collective-permute-start(bf16[7,288,128]{2,1,0:T(8,128)(2,1)S(1)} %pad_maximum_fusion.1), channel_id=1, source_target_pairs={{4,0},{8,4},{12,8},{5,1},{9,5},{13,9},{6,2},{10,6},{14,10},{7,3},{... | collective-permute-start | bytes 1548296 | tf_op jit(solution)/shard_map/ppermute | solution.py:639
  19.1 4.2 %copy-start.3 = (bf16[7,288,128]{2,1,0:T(8,128)(2,1)}, bf16[7,288,128]{2,1,0:T(8,128)(2,1)S(1)}, u32[]{:S(2)}) copy-start(bf16[7,288,128]{2,1,0:T(8,128)(2,1)S(1)} %collective-permute-done.before) | copy-start | bytes 1548292
  23.3 0.8 copy-start.4
  59.1 80.1 %copy-start.1 = (f32[288,288]{1,0:T(8,128)S(1)}, f32[288,288]{1,0:T(8,128)}, u32[]{:S(2)}) copy-start(f32[288,288]{1,0:T(8,128)} %constant.82.clone.cas_across) | copy-start | bytes 995332
  59.1 80.1 %copy-start.2 = (f32[128,128]{1,0:T(8,128)S(1)}, f32[128,128]{1,0:T(8,128)}, u32[]{:S(2)}) copy-start(f32[128,128]{1,0:T(8,128)} %constant.81.clone.cas.cas_depth) | copy-start | bytes 196612
  139.2 1.5 copy-start
where the time goes:
time: 185 us; the launch traced here: 183 us
  Pallas kernels  156 us (84%)
  waiting for transfers between devices  11.2 us (6%)
  local copies, waits for them, and re-layouts  6.61 us (4%)
  starting transfers between devices  6.25 us (3%)
  other arithmetic  2.01 us (1%)
    pallas_call x1, Pallas kernels, fast(): pl.pallas_call(gradient_kernel, out_shape=shape(groups, width, depth), in...  80 us
    pallas_call x1, Pallas kernels, fast(): pl.pallas_call(spectral_kernel, out_shape=shape(rows, part, depth), in_sp...  41.3 us
    pallas_call x1, Pallas kernels, fast(): pl.pallas_call(residual_kernel, out_shape=[shape(rows + 4, width, depth),...  34.9 us
    ppermute x1, waiting for transfers between devices, fast(): before = lax.ppermute(high, 'space', [(i, i + 1) for i in range(slabs - 1)])  7.01 us
    ppermute x1, starting transfers between devices, fast(): before = lax.ppermute(high, 'space', [(i, i + 1) for i in range(slabs - 1)])  4.96 us
    ppermute x1, waiting for transfers between devices, fast(): after = lax.ppermute(low, 'space', [(i + 1, i) for i in range(slabs - 1)])  4.22 us
  transfers between devices with their start and end apart: 2, of which 2 were waited for; matrix products, arithmetic and copies ran while one was open for 1% of the time, Pallas kernels for 0%

commit v1 on v0

v1 whole, which is shorter than its diff:
```python
import jax
import jax.numpy as jnp
import numpy as np
from jax import lax
from jax.experimental import pallas as pl
from jax.experimental.pallas import tpu as pltpu
from jax.sharding import PartitionSpec as P

ITERS = 2


prior_gain = 5.0
range_squared = 4.0


def with_halo(cells, sides, width):
    for axis, dim in sides:
        count = lax.axis_size(axis)
        ends = count - 1
        head = lax.slice_in_dim(cells, 0, width, axis=dim)
        tail = lax.slice_in_dim(cells, cells.shape[dim] - width, cells.shape[dim], axis=dim)
        cells = jnp.concatenate(
            [
                lax.ppermute(tail, axis, [(i, (i + 1) % count) for i in range(ends)]),
                cells,
                lax.ppermute(head, axis, [((i + 1) % count, i) for i in range(ends)]),
            ],
            axis=dim,
        )
    return cells


def neighbours(padded):
    return [
        padded[2:, 1:-1, 1:-1],
        padded[:-2, 1:-1, 1:-1],
        padded[1:-1, 2:, 1:-1],
        padded[1:-1, :-2, 1:-1],
        padded[1:-1, 1:-1, 2:],
        padded[1:-1, 1:-1, :-2],
    ]


def operate(values, padded, conduct):
    summed = jnp.zeros_like(values)
    for face_k, beside in zip(conduct, neighbours(padded)):
        summed = summed + face_k * (values - beside)
    return summed


def kappa_of(indices, length):
    return 4.0 * jnp.sin(jnp.pi * indices / length) ** 2


def pad_sides(padded):
    return jnp.pad(padded, ((0, 0), (1, 1), (1, 1)))


def with_faces(values):
    return pad_sides(with_halo(values, (("space", 0),), 1))


def squares(residual):
    return lax.psum(jnp.sum(residual * residual), "space")


def hartley(length):
    indices = jnp.arange(length, dtype=jnp.int32)
    products = indices[:, None] * indices[None, :] % length
    angles = products.astype(jnp.float32) * (2.0 * jnp.pi / length)
    return jnp.cos(angles) + jnp.sin(angles)


def on_device(log_k, heads, warm_adjoint, obs_columns, obs_residuals, well_columns):
    slab_rows, width_cells, depth_cells = log_k.shape
    space_count = lax.axis_size("space")
    first_row = lax.axis_index("space") * slab_rows
    logk_pad, head_pad = (
        with_halo(log_k, (("space", 0),), 1),
        with_halo(heads[0], (("space", 0),), 1),
    )
    logk_val = log_k.astype(jnp.float32)
    conduct = [
        jnp.exp(0.5 * (logk_val + beside))
        for beside in neighbours(pad_sides(logk_pad.astype(jnp.float32)))
    ]
    columns = obs_columns[0]
    row_local = columns // width_cells - first_row
    inside = (row_local >= 0) & (row_local < slab_rows)
    row_local = jnp.where(inside, row_local, slab_rows)
    source = jnp.zeros((slab_rows, width_cells, depth_cells), jnp.float32)
    source = source.at[row_local, columns % width_cells].add(obs_residuals[0], mode="drop")
    adjoint = warm_adjoint[0].astype(jnp.float32)
    lam_padded = with_faces(adjoint)
    residual = source - operate(adjoint, lam_padded, conduct)
    direction = residual
    norm_now = squares(residual)
    for iteration in range(ITERS):
        dir_padded = with_faces(direction)
        applied = operate(direction, dir_padded, conduct)
        step_length = norm_now / lax.psum(jnp.sum(direction * applied), "space")
        adjoint = adjoint + step_length * direction
        lam_padded = lam_padded + step_length * dir_padded
        if iteration + 1 < ITERS:
            residual = residual - step_length * applied
            norm_next = squares(residual)
            direction = residual + norm_next / norm_now * direction
            norm_now = norm_next
    lam_full = pad_sides(with_halo(adjoint, (("space", 0),), 1))
    head_val = heads[0].astype(jnp.float32)
    misfit_term = jnp.zeros_like(adjoint)
    for face_k, lam_side, head_side in zip(
        conduct, neighbours(lam_full), neighbours(pad_sides(head_pad.astype(jnp.float32)))
    ):
        misfit_term = misfit_term + face_k * (adjoint - lam_side) * (head_val - head_side)
    column_ids = (first_row + jnp.arange(slab_rows, dtype=jnp.int32))[
        :, None
    ] * width_cells + jnp.arange(width_cells, dtype=jnp.int32)[None, :]
    keep_mask = (column_ids != well_columns[0]).astype(jnp.float32)
    partial_value = -0.5 * misfit_term * keep_mask[:, :, None]
    highest = lax.Precision.HIGHEST
    cas_depth = hartley(depth_cells)
    cas_across = hartley(width_cells)
    along_cells = slab_rows * space_count
    cas_along = hartley(along_cells)
    summed = lax.psum_scatter(partial_value, "test", scatter_dimension=1, tiled=True)
    depth_freq = jnp.einsum("xyz,zk->xky", summed, cas_depth, precision=highest)
    pencil = lax.all_to_all(depth_freq, "test", split_axis=1, concat_axis=2, tiled=True)
    across_freq = jnp.einsum("xzy,yk->kzx", pencil, cas_across, precision=highest)
    column_block = lax.all_to_all(across_freq, "space", split_axis=0, concat_axis=2, tiled=True)
    along_freq = jnp.einsum("yzx,xk->yzk", column_block, cas_along, precision=highest)
    across_rows = column_block.shape[0]
    depth_rows = column_block.shape[1]
    kappa_x = kappa_of(jnp.arange(along_cells).astype(jnp.float32), along_cells)
    kappa_y = kappa_of(
        (lax.axis_index("space") * across_rows + jnp.arange(across_rows)).astype(jnp.float32),
        width_cells,
    )
    kappa_z = kappa_of(
        (lax.axis_index("test") * depth_rows + jnp.arange(depth_rows)).astype(jnp.float32),
        depth_cells,
    )
    spectrum = (
        prior_gain
        / (
            1.0
            + range_squared
            * (kappa_y[:, None, None] + kappa_z[None, :, None] + kappa_x[None, None, :])
        )
        ** 2
    )
    along_back = jnp.einsum("yzk,kx->yzx", along_freq * spectrum, cas_along, precision=highest)
    slab_block = lax.all_to_all(along_back, "space", split_axis=2, concat_axis=0, tiled=True)
    across_back = jnp.einsum("yzx,yk->xzk", slab_block, cas_across, precision=highest)
    depth_block = lax.all_to_all(across_back, "test", split_axis=2, concat_axis=1, tiled=True)
    result = jnp.einsum("xky,kz->xyz", depth_block, cas_depth, precision=highest)
    scale_back = 1.0 / (along_cells * width_cells * depth_cells)
    return result * scale_back


GUARD = 8
STEP = 256.0
TOP = 32000.0
BF = jnp.bfloat16
F32 = jnp.float32
VM = pl.BlockSpec(memory_space=pltpu.VMEM)
SM = pl.BlockSpec(memory_space=pltpu.SMEM)
ANY = pl.BlockSpec(memory_space=pl.ANY)
MESH = pl.DeviceIdType.MESH


def shape(*dims, dtype=jnp.float32):
    return jax.ShapeDtypeStruct(dims, dtype)


def iota(plane, axis):
    return lax.broadcasted_iota(jnp.int32, plane, axis)


def halves(values):
    top = values.astype(BF)
    return top, (values - top.astype(F32)).astype(BF)


def matmul(a, b):
    return jnp.dot(a, b, preferred_element_type=F32)


def dot3(a, b):
    a_top, a_low = halves(a)
    b_top, b_low = halves(b)
    return matmul(a_top, b_top) + (matmul(a_top, b_low) + matmul(a_low, b_top))


def encode(values, spare):
    rows, lanes = values.shape
    peak = jnp.maximum(jnp.max(jnp.abs(values), axis=0, keepdims=True), 1e-30)
    level = jnp.ceil(jnp.log2(peak) * STEP)
    scaled = jnp.round(values * (jnp.exp2(level * (-1.0 / STEP)) * TOP))
    both = jnp.concatenate([scaled, jnp.broadcast_to(level, (spare, lanes))], axis=0)
    return both.astype(jnp.int32).astype(jnp.int16)


def decode(codes, spare):
    wide = codes.astype(jnp.int32).astype(F32)
    rows = wide.shape[0] - spare
    level = wide[rows : rows + 1]
    return wide[:rows] * (jnp.exp2(level * (1.0 / STEP)) * (1.0 / TOP))


def swap_blocks(planes):
    count = len(planes)
    lanes = planes[0].shape[1]
    block = lanes // count
    at_lane = iota(planes[0].shape, 1) // block
    swapped = []
    for to in range(count):
        joined = planes[to]
        for frm in range(count):
            if frm != to:
                shift = (block * (frm - to)) % lanes
                joined = jnp.where(at_lane == frm, pltpu.roll(planes[frm], shift, 1), joined)
        swapped.append(joined)
    return swapped


def greet(others):
    barrier = pltpu.get_barrier_semaphore()
    for other in others:
        pl.semaphore_signal(barrier, inc=1, device_id=other, device_id_type=MESH)
    pl.semaphore_wait(barrier, len(others))


def gradient_kernel(
    well,
    columns,
    observed,
    logk,
    warm,
    heads,
    turned,
    out,
    lk,
    wm,
    hd,
    soft,
    res,
    img,
    ring,
    sources,
    acc,
    shared,
    mine,
    from_mate,
    ship,
    got,
    load_sem,
    halo_send,
    halo_take,
    send_sum,
    take_sum,
    send_mate,
    take_mate,
    send_across,
    take_across,
):
    rows, width, depth = logk.shape
    parts = 4
    chunk = rows // parts
    piece = width // 3
    pieces = range(3)
    slabs = shared.shape[0]
    slab, here = lax.axis_index("space"), lax.axis_index("test")
    half, core = here // 2, lax.rem(here, 2)
    mate = {"test": 2 * half + 1 - core}
    across = {"test": 2 * (1 - half) + core}
    others = [{"space": lax.rem(slab + k, slabs)} for k in range(1, slabs)]
    first_row = slab * rows

    def loads(m):
        span = pl.ds(m * chunk, chunk)
        to = pl.ds(3 + m * chunk, chunk)
        return [
            pltpu.make_async_copy(frm.at[span], held.at[to], load_sem.at[n, m])
            for n, (frm, held) in enumerate(((logk, lk), (warm, wm), (heads, hd)))
        ]

    for m in range(parts):
        for copy in loads(m):
            copy.start()

    def halo(direction):
        up = direction == 1
        copies = []
        for n, (frm, held, deep) in enumerate(((logk, lk, 3), (warm, wm, 3), (heads, hd, 1))):
            at = rows - deep if up else 0
            to = 3 - deep if up else 3 + rows
            copies.append(
                pltpu.make_async_remote_copy(
                    src_ref=frm.at[pl.ds(at, deep)],
                    dst_ref=held.at[pl.ds(to, deep)],
                    send_sem=halo_send.at[direction, n],
                    recv_sem=halo_take.at[direction, n],
                    device_id={"space": slab + 1 if up else slab - 1},
                    device_id_type=MESH,
                )
            )
        return copies

    greet(others + [mate, across])

    @pl.when(slab > 0)
    def _():
        for copy in halo(0):
            copy.start()

    @pl.when(slab < slabs - 1)
    def _():
        for copy in halo(1):
            copy.start()

    blank = jnp.zeros((3, width, depth), BF)

    @pl.when(slab == 0)
    def _():
        lk[0:3] = blank
        wm[0:3] = blank
        hd[0:3] = blank

    @pl.when(slab == slabs - 1)
    def _():
        lk[rows + 3 : rows + 6] = blank
        wm[rows + 3 : rows + 6] = blank
        hd[rows + 3 : rows + 6] = blank

    top, low = halves(observed[...])
    sources[...] = jnp.concatenate([top, low], axis=0)
    acc[...] = jnp.zeros_like(acc)
    edge = jnp.zeros((GUARD, depth), F32)
    for i in range(ring.shape[0]):
        ring[i, 0:GUARD, :] = edge
        ring[i, width + GUARD : width + 2 * GUARD, :] = edge

    at_lane = iota((piece, depth), 1)
    at_row = iota((piece, depth), 0)
    is_first, is_last = at_lane == 0, at_lane == depth - 1
    spots = iota((piece, columns.shape[1]), 0)

    def at(c):
        return pl.ds(c * piece, piece)

    def near(ref, i, c, off=0):
        return ref[i, pl.ds(GUARD + c * piece + off, piece), :]

    def store(ref, i, c, value):
        ref[i, pl.ds(GUARD + c * piece, piece), :] = value

    def ahead(value):
        return pltpu.roll(value, depth - 1, 1)

    def behind(value):
        return pltpu.roll(value, 1, 1)

    def beside(ref, below, i, above, c, outer):
        held = near(ref, i, c)
        lanes = jnp.where(is_last, outer, ahead(held)) + jnp.where(is_first, outer, behind(held))
        ends = near(ref, i, c, -1) + near(ref, i, c, 1)
        return held, (lanes + ends) + (near(ref, below, c) + near(ref, above, c))

    def partial(value):
        return jnp.sum(value.reshape(piece // 8, 8, depth), axis=0)

    def slot(n, base):
        return base + lax.rem(n, 4)

    def outside(n):
        return jnp.logical_or(
            jnp.logical_and(slab == 0, n < 3), jnp.logical_and(slab == slabs - 1, n >= rows + 3)
        )

    def prepare(n):
        one = jnp.ones((GUARD, depth), F32)
        soft[n, 0:GUARD, :] = one
        soft[n, width + GUARD : width + 2 * GUARD, :] = one
        for c in pieces:
            value = jnp.exp(0.5 * lk[n, at(c), :].astype(F32))
            store(soft, n, c, value)
            store(ring, slot(n, 0), c, value * wm[n, at(c), :].astype(F32))

    def residual(n):
        spot = columns[...] - (first_row + n - 3) * width
        for c in pieces:
            s, around = beside(soft, n - 1, n, n + 1, c, 1.0)
            held, total = beside(ring, slot(n - 1, 0), slot(n, 0), slot(n + 1, 0), c, 0.0)
            hits = jnp.where(spots == spot - c * piece, 1.0, 0.0).astype(BF)
            value = (s * total - held * around) + matmul(hits, sources[...])
            res[n, at(c), :] = value
            store(ring, slot(n, 4), c, s * value)
            store(ring, slot(n, 12), c, around)

        @pl.when(outside(n))
        def _():
            for c in pieces:
                res[n, at(c), :] = jnp.zeros((piece, depth), F32)
                store(ring, slot(n, 4), c, jnp.zeros((piece, depth), F32))

    def image(n, own):
        for c in pieces:
            held, total = beside(ring, slot(n - 1, 4), slot(n, 4), slot(n + 1, 4), c, 0.0)
            s, value = near(soft, n, c), res[n, at(c), :]
            applied = held * near(ring, slot(n, 12), c) - s * total
            img[n, at(c), :] = applied
            store(ring, slot(n, 8), c, s * applied)
            acc[0] += own * partial(value * value)
            acc[1] += own * partial(value * applied)

        @pl.when(outside(n))
        def _():
            for c in pieces:
                img[n, at(c), :] = jnp.zeros((piece, depth), F32)
                store(ring, slot(n, 8), c, jnp.zeros((piece, depth), F32))

    def twice(n):
        for c in pieces:
            held, total = beside(ring, slot(n - 1, 8), slot(n, 8), slot(n + 1, 8), c, 0.0)
            value = img[n, at(c), :]
            acc[2] += partial(value * value)
            acc[3] += partial(held * (value * near(ring, slot(n, 12), c) - total))

    def sweep(first, last, least, most):
        def step(k, _):
            if first == 3:

                @pl.when(jnp.logical_and(lax.rem(k - 3, chunk) == 0, k < rows + 3))
                def _():
                    for copy in loads((k - 3) // chunk):
                        copy.wait()

                @pl.when(jnp.logical_and(k == rows + 3, slab < slabs - 1))
                def _():
                    for copy in halo(0):
                        copy.wait_recv()

            prepare(k)

            @pl.when(k >= first + 2)
            def _():
                residual(k - 1)

            @pl.when(k >= first + 4)
            def _():
                own = jnp.logical_and(k - 2 >= least, k - 2 <= most)
                image(k - 2, own.astype(F32))

            @pl.when(k >= first + 6)
            def _():
                twice(k - 3)

            return 0

        lax.fori_loop(first, last + 1, step, 0)

    sweep(3, rows + 5, 5, rows + 2)

    @pl.when(slab > 0)
    def _():
        for copy in halo(1):
            copy.wait_recv()

    sweep(0, 8, 3, 4)

    shared[slab] = acc[...]
    copies = [
        pltpu.make_async_remote_copy(
            src_ref=shared.at[slab],
            dst_ref=shared.at[slab],
            send_sem=send_sum.at[k],
            recv_sem=take_sum.at[k],
            device_id=other,
            device_id_type=MESH,
        )
        for k, other in enumerate(others)
    ]
    for copy in copies:
        copy.start()

    @pl.when(slab > 0)
    def _():
        for copy in halo(0):
            copy.wait_send()

    @pl.when(slab < slabs - 1)
    def _():
        for copy in halo(1):
            copy.wait_send()

    for copy in copies:
        copy.wait()

    def gathered(n):
        total = shared[0, n]
        for m in range(1, slabs):
            total = total + shared[m, n]
        return jnp.broadcast_to(jnp.sum(total, axis=(0, 1), keepdims=True), (1, depth))

    norm, curve, square, bend = [gathered(n) for n in range(4)]
    length = norm / curve
    norm_next = length * length * square - norm
    curve_next = curve - 2.0 * length * square + length * length * bend
    ratio = norm_next / norm
    length_next = norm_next / (curve_next - ratio * norm_next / length)
    with_start = length + length_next * (1.0 + ratio)
    with_image = length_next * length

    def eighth(n, base):
        return base + lax.rem(n, 8)

    def fill(n):
        for c in pieces:
            field = wm[n, at(c), :].astype(F32)
            field = field + (with_start * res[n, at(c), :] - with_image * img[n, at(c), :])
            store(ring, eighth(n, 0), c, field)
            store(ring, eighth(n, 8), c, hd[n, at(c), :].astype(F32))

    fill(2)
    fill(3)
    count = 4
    groups = rows // count
    at_block = at_lane // (depth // count)

    def group(g):
        start = 3 + count * g
        for p in range(count):
            fill(start + p + 1)
        for c in pieces:
            fields = [near(ring, eighth(start + p, 0), c) for p in range(-1, count + 1)]
            levels = [near(ring, eighth(start + p, 8), c) for p in range(-1, count + 1)]
            steps = [
                (fields[p] - fields[p + 1]) * (levels[p] - levels[p + 1]) for p in range(count + 1)
            ]
            turns = []
            for p in range(count):
                n = start + p
                f, h, s = fields[p + 1], levels[p + 1], near(soft, n, c)
                total = near(soft, n - 1, c) * steps[p] + near(soft, n + 1, c) * steps[p + 1]
                for off in (-1, 1):
                    field = near(ring, eighth(n, 0), c, off)
                    level = near(ring, eighth(n, 8), c, off)
                    total += near(soft, n, c, off) * ((f - field) * (h - level))
                both = f * h
                product = (f - ahead(f)) * (h - ahead(h))
                total += jnp.where(is_last, both, ahead(s) * product)
                total += jnp.where(is_first, both, behind(s * product))
                place = well[0] - (first_row + n - 3) * width - c * piece
                value = jnp.where(at_row != place, s * total, 0.0)
                double = matmul(jnp.concatenate(halves(value), axis=1), turned[p])
                turns.append(double[:, :depth] + double[:, depth:])
            for t in range(count):
                joined = turns[-t % count]
                for b in range(1, count):
                    joined = jnp.where(at_block == b, turns[(b - t) % count], joined)
                mine[t % 2, g, t // 2, at(c), :] = joined
        to_mate(g).start()

    def to_mate(g):
        return pltpu.make_async_remote_copy(
            src_ref=mine.at[1 - core, g],
            dst_ref=from_mate.at[g],
            send_sem=send_mate.at[g],
            recv_sem=take_mate.at[g],
            device_id=mate,
            device_id_type=MESH,
        )

    def to_across(g):
        return pltpu.make_async_remote_copy(
            src_ref=ship.at[g],
            dst_ref=got.at[g],
            send_sem=send_across.at[g],
            recv_sem=take_across.at[g],
            device_id=across,
            device_id_type=MESH,
        )

    def relay(g):
        to_mate(g).wait_recv()
        ship[g] = encode(mine[core, g, 1 - half] + from_mate[g, 1 - half], 16)
        to_across(g).start()

    group(0)

    def step(g, _):
        group(g)
        relay(g - 1)
        return 0

    lax.fori_loop(1, groups, step, 0)
    relay(groups - 1)

    def finish(g, _):
        to_across(g).wait_recv()
        out[g] = (mine[core, g, half] + from_mate[g, half]) + decode(got[g], 16)
        to_mate(g).wait_send()
        to_across(g).wait_send()
        return 0

    lax.fori_loop(0, groups, finish, 0)


def spectral_kernel(
    summed,
    listed,
    cas_across,
    cas_depth,
    out,
    tables,
    freq,
    moments,
    filtered,
    going,
    coming,
    load_sem,
    send_end,
    take_end,
    send_back,
    take_back,
):
    groups, width, lanes = summed.shape
    count, part = going.shape[0], width // going.shape[0]
    spare = going.shape[2] - part
    rows = groups * count
    slabs = moments.shape[0]
    slab, here = lax.axis_index("space"), lax.axis_index("test")
    others = [{"space": lax.rem(slab + k, slabs)} for k in range(1, slabs)]
    peers = [lax.rem(here + k, count) for k in range(1, count)]
    fetch = pltpu.make_async_copy(listed.at[here], tables, load_sem)
    fetch.start()
    greet(others + [{"test": peer} for peer in peers])
    turn = lax.rem((count - here) * (lanes // count), lanes)

    def mix(g, _):
        top, low = halves(pltpu.roll(summed[g], turn, 1))
        mixed = matmul(cas_across[...], jnp.concatenate([top, top, low], axis=0))
        blocks = [mixed[j * part : (j + 1) * part] for j in range(count)]
        for p, plane in enumerate(swap_blocks(blocks)):
            freq[g * count + p] = plane
        return 0

    lax.fori_loop(0, groups, mix, 0)
    fetch.wait()
    pole, level, slope, decay, wrap_one, wrap_two = (tables[n] for n in range(6))

    def walk(i, carry):
        one, two, back_one, back_two = carry
        value, back = freq[i], freq[rows - 1 - i]
        return (
            value + pole * one,
            pole * (two + one),
            back + pole * back_one,
            pole * (back_two + back_one),
        )

    zero = jnp.zeros((part, lanes), jnp.float32)
    ends = lax.fori_loop(0, rows, walk, (zero, zero, zero, zero))
    for n in range(4):
        moments[slab, n] = encode(ends[n], spare)
    copies = [
        pltpu.make_async_remote_copy(
            src_ref=moments.at[slab],
            dst_ref=moments.at[slab],
            send_sem=send_end.at[k],
            recv_sem=take_end.at[k],
            device_id=other,
            device_id_type=MESH,
        )
        for k, other in enumerate(others)
    ]
    for copy in copies:
        copy.start()
    for copy in copies:
        copy.wait()

    def carried(direction, n):
        one, two = zero, zero
        for m in range(slabs, 0, -1):
            other = lax.rem(slab + 2 * slabs - direction * m, slabs)
            one, two = (
                decay * one + decode(moments[other, n], spare),
                decay * (two + rows * one) + decode(moments[other, n + 1], spare),
            )
        return wrap_one * one, wrap_one * two + wrap_two * one

    def forward(i, carry):
        one, two = carry
        two = pole * (two + one)
        one = freq[i] + pole * one
        filtered[i] = level * one + slope * two
        return one, two

    lax.fori_loop(0, rows, forward, carried(1, 0))

    def backward(i, carry):
        one, two = carry
        at = rows - 1 - i
        two = pole * (two + one)
        one = pole * one
        filtered[at] += level * one + slope * two
        return one + freq[at], two

    lax.fori_loop(0, rows, backward, carried(-1, 2))

    def to_peer(k, g):
        return pltpu.make_async_remote_copy(
            src_ref=going.at[peers[k], g],
            dst_ref=coming.at[here, g],
            send_sem=send_back.at[k, g],
            recv_sem=take_back.at[k, g],
            device_id={"test": peers[k]},
            device_id_type=MESH,
        )

    def unmix(g, _):
        blocks = swap_blocks([filtered[g * count + p] for p in range(count)])
        top, low = halves(jnp.concatenate(blocks, axis=0))
        mixed = matmul(cas_across[...], jnp.concatenate([top, top, low], axis=0))
        for u in range(count):
            going[u, g] = encode(mixed[u * part : (u + 1) * part], spare)
        for k in range(count - 1):
            to_peer(k, g).start()
        coming[here, g] = going[here, g]
        return 0

    lax.fori_loop(0, groups, unmix, 0)

    def back(g, _):
        for k in range(count - 1):
            to_peer(k, g).wait()
        planes = [decode(coming[t, g], spare) for t in range(count)]
        for p, plane in enumerate(swap_blocks(planes)):
            out[g * count + p] = dot3(plane, cas_depth[...])
        return 0

    lax.fori_loop(0, groups, back, 0)


def table(length):
    indices = np.arange(length)
    angles = (indices[:, None] * indices[None, :] % length) * (2.0 * np.pi / length)
    return (np.cos(angles) + np.sin(angles)).astype(np.float32)


def split(values):
    top = values.astype(jnp.bfloat16)
    return top, (values - top.astype(np.float32)).astype(jnp.bfloat16)


def turned_tables(length, count):
    tables = []
    for p in range(count):
        top, low = split(-0.5 * np.roll(table(length), p * (length // count), axis=1))
        tables.append(np.block([[top, low], [top, np.zeros_like(low)]]))
    return np.stack(tables)


def filter_tables(rows, along, width, depth, count):
    def kappa(length):
        return 4.0 * np.sin(np.pi * np.arange(length) / length) ** 2

    part, block = width // count, depth // count
    lanes_at = np.arange(depth)
    across_at = (lanes_at // block)[None, :] * part + np.arange(part)[:, None]
    listed = []
    for here in range(count):
        depth_at = here * block + lanes_at % block
        shift = 1.0 + range_squared * (kappa(width)[across_at] + kappa(depth)[depth_at][None, :])
        centre = 1.0 + shift / (2.0 * range_squared)
        pole = 1.0 / (centre + np.sqrt(centre * centre - 1.0))
        square = pole * pole
        gain = prior_gain / (range_squared * range_squared) * square / (width * depth)
        slope = gain / (1.0 - square) ** 2
        level = slope * (1.0 + square) / (1.0 - square)
        turn = pole**along
        wrap_one = 1.0 / (1.0 - turn)
        wrap_two = along * turn * wrap_one * wrap_one
        listed.append(np.stack([pole, level, slope, pole**rows, wrap_one, wrap_two]))
    return np.stack(listed).astype(np.float32)


def fast(log_k, heads, warm_adjoint, obs_columns, obs_residuals, well_columns):
    rows, width, depth = log_k.shape
    slabs = lax.axis_size("space")
    count = lax.axis_size("test")
    part = width // count
    groups = rows // count
    observed = obs_columns.shape[1]
    planes = rows + 6
    padded = width + 2 * GUARD
    spare = 16 - part % 16
    summed = pl.pallas_call(
        gradient_kernel,
        out_shape=shape(groups, width, depth),
        in_specs=[SM, VM, VM, ANY, ANY, ANY, VM],
        out_specs=VM,
        scratch_shapes=[pltpu.VMEM((planes, width, depth), BF)] * 3
        + [
            pltpu.VMEM((planes, padded, depth), F32),
            pltpu.VMEM((planes, width, depth), F32),
            pltpu.VMEM((planes, width, depth), F32),
            pltpu.VMEM((16, padded, depth), F32),
            pltpu.VMEM((2 * observed, depth), BF),
            pltpu.VMEM((4, 8, depth), F32),
            pltpu.VMEM((slabs, 4, 8, depth), F32),
            pltpu.VMEM((2, groups, 2, width, depth), F32),
            pltpu.VMEM((groups, 2, width, depth), F32),
            pltpu.VMEM((groups, width + 16, depth), jnp.int16),
            pltpu.VMEM((groups, width + 16, depth), jnp.int16),
            pltpu.SemaphoreType.DMA((3, 4)),
        ]
        + [pltpu.SemaphoreType.DMA((2, 3))] * 2
        + [pltpu.SemaphoreType.DMA((slabs - 1,))] * 2
        + [pltpu.SemaphoreType.DMA((groups,))] * 4,
        compiler_params=pltpu.CompilerParams(
            vmem_limit_bytes=60 * 1024 * 1024, collective_id=1, has_side_effects=True
        ),
        name="gradient",
    )(
        well_columns,
        jnp.concatenate([obs_columns, obs_columns], axis=1),
        obs_residuals[0],
        log_k,
        warm_adjoint[0],
        heads[0],
        jnp.asarray(turned_tables(depth, count)),
    )
    top, low = split(table(width))
    return pl.pallas_call(
        spectral_kernel,
        out_shape=shape(rows, part, depth),
        in_specs=[VM, ANY, VM, VM],
        out_specs=VM,
        scratch_shapes=[
            pltpu.VMEM((6, part, depth), F32),
            pltpu.VMEM((rows, part, depth), F32),
            pltpu.VMEM((slabs, 4, part + spare, depth), jnp.int16),
            pltpu.VMEM((rows, part, depth), F32),
            pltpu.VMEM((count, groups, part + spare, depth), jnp.int16),
            pltpu.VMEM((count, groups, part + spare, depth), jnp.int16),
            pltpu.SemaphoreType.DMA,
            pltpu.SemaphoreType.DMA((slabs - 1,)),
            pltpu.SemaphoreType.DMA((slabs - 1,)),
            pltpu.SemaphoreType.DMA((count - 1, groups)),
            pltpu.SemaphoreType.DMA((count - 1, groups)),
        ],
        compiler_params=pltpu.CompilerParams(
            vmem_limit_bytes=40 * 1024 * 1024, collective_id=2, has_side_effects=True
        ),
        name="spectral",
    )(
        summed,
        jnp.asarray(filter_tables(rows, rows * slabs, width, depth, count)),
        jnp.asarray(np.concatenate([top, low, top], axis=1)),
        jnp.asarray(table(depth)),
    )


def pick(log_k, heads, warm_adjoint, obs_columns, *rest):
    rows, width, depth = log_k.shape
    count = lax.axis_size("test")
    fits = depth == 128 and count == 4 and rows % 4 == 0 and rows >= 12 and width % 96 == 0
    fits = fits and obs_columns.shape[1] % 64 == 0 and rows * width <= 48 * 288
    run = fast if fits and lax.axis_size("space") > 1 else on_device
    return run(log_k, heads, warm_adjoint, obs_columns, *rest)


def solution(mesh):
    placed = (
        P(("groups", "space"), None, None),
        P("test", ("groups", "space"), None, None),
        P("test", ("groups", "space"), None, None),
        P("test", "groups"),
        P("test", "groups", None),
        P(("groups", "test")),
    )
    return jax.shard_map(
        pick,
        mesh=mesh,
        in_specs=placed,
        out_specs=P(("groups", "space"), "test", None),
        check_vma=False,
    )
```

time: 185 us -> 110 us (0.59)
  Pallas kernels: 156 us -> 105 us
  waiting for transfers between devices: 11.2 us -> 0 us
  starting transfers between devices: 6.25 us -> 0 us
  local copies, waits for them, and re-layouts: 6.61 us -> 2.69 us
    pallas_call x1 -> x0, Pallas kernels: 34.9 us -> none  [fast(): pl.pallas_call(residual_kernel, out_shape=[shape(rows + 4, width, depth),...]
    ppermute x2 -> x0, waiting for transfers between devices: 11.2 us -> none  [the longest x1 7.01 us: fast(): before = lax.ppermute(high, 'space', [(i, i + 1) for i in range(slabs - 1)])]
    pallas_call x1, Pallas kernels: 41.3 us -> 30.9 us  [fast(): pl.pallas_call(spectral_kernel, out_shape=shape(rows, part, depth), in_sp...]
    ppermute x2 -> x0, starting transfers between devices: 6.25 us -> none  [the longest x1 4.96 us: fast(): before = lax.ppermute(high, 'space', [(i, i + 1) for i in range(slabs - 1)])]
    pallas_call x1, Pallas kernels: 80 us -> 74.2 us  [fast(): pl.pallas_call(gradient_kernel, out_shape=shape(groups, width, depth), in...]
    slice x3 -> x0, local copies, waits for them, and re-layouts: 3.08 us -> none  [fast(): low = jnp.concatenate([log_k[:3], warm[:3], head[:1]])]
  transfers between devices with their start and end apart: 2 -> 0, of which waited for: 2 -> 0; matrix products, arithmetic and copies ran while one was open for 1% -> 0% of each run, Pallas kernels for 0% -> 0%
where the time goes in v1:
time: 110 us
  Pallas kernels  105 us (95%)
  local copies, waits for them, and re-layouts  2.69 us (2%)
  other arithmetic  1.31 us (1%)
    pallas_call x1, Pallas kernels, fast(): pl.pallas_call(gradient_kernel, out_shape=shape(groups, width, depth), in...  74.2 us
    pallas_call x1, Pallas kernels, fast(): pl.pallas_call(spectral_kernel, out_shape=shape(rows, part, depth), in_sp...  30.9 us
    unnamed x9, local copies, waits for them, and re-layouts  2.69 us

profile of v1, /device:TPU:0, one launch (start us, length us, event | category | flops | bytes accessed | tf_op | source)
XLA Modules:
  0.0 109.8 jit_solution(16916177608550067829)
XLA Ops:
  0.7 1.3 %pad_add_fusion.columns = s32[1,128]{1,0:T(1,128)} fusion(s32[1,64]{1,0:T(1,128)} %param.13), kind=kLoop, calls=%fused_computation | loop fusion | flops 128 | bytes 768 | tf_op jit(solution)/shard_map/concatenate | solution.py:828
  2.0 0.0 copy-start.1
  2.0 0.0 copy-start.2
  2.0 0.0 copy-start.3
  2.0 74.2 %gradient.1.summed = f32[12,288,128]{2,1,0:T(8,128)} custom-call(s32[1]{0:T(128)S(6)} %copy.12.well, s32[1,128]{1,0:T(1,128)} %pad_add_fusion.columns, f32[64,128]{1,0:T(8,128)} %bitcast.5, bf16[48,288,128]{2,1,0:T(8,128)(2,1)} %logk.1, bf16[48,288,128]{2,1,0:T(8,128)(2,1)} %bitcast.3, bf16[48,288,128]{2,1,0:T(8,128)(2,1)} %bitcast.4, ...), custom_call_target="tpu_custom_call" | custom-call | tf_op jit(solution)/shard_map/gradient/pallas_call | solution.py:799
  76.2 0.0 copy-done.1
  76.2 0.0 copy-done.2
  76.2 0.0 copy-done.3
  76.2 0.0 copy-start
  76.2 1.5 %copy-done = f32[12,288,128]{2,1,0:T(8,128)S(1)} copy-done((f32[12,288,128]{2,1,0:T(8,128)S(1)}, f32[12,288,128]{2,1,0:T(8,128)}, u32[]{:S(2)}) %copy-start) | copy-done | bytes 1769496
  77.7 30.9 %spectral.1 = f32[48,72,128]{2,1,0:T(8,128)S(1)} custom-call(f32[12,288,128]{2,1,0:T(8,128)S(1)} %copy-done, f32[4,6,72,128]{3,2,1,0:T(8,128)S(1)} %copy-done.1, bf16[288,864]{1,0:T(8,128)(2,1)S(1)} %copy-done.2, f32[128,128]{1,0:T(8,128)S(1)} %copy-done.3), custom_call_target="tpu_custom_call" | custom-call | tf_op jit(solution)/shard_map/spectral/pallas_call | solution.py:836
  108.6 1.2 %copy.13 = f32[48,72,128]{2,1,0:T(8,128)} copy(f32[48,72,128]{2,1,0:T(8,128)S(1)} %spectral.1) | data formatting | bytes 3538944
Async XLA Ops:
  2.0 74.2 %copy-start.1 = (f32[4,6,72,128]{3,2,1,0:T(8,128)S(1)}, f32[4,6,72,128]{3,2,1,0:T(8,128)}, u32[]{:S(2)}) copy-start(f32[4,6,72,128]{3,2,1,0:T(8,128)} %constant.9.clone.listed) | copy-start | bytes 2654212
  2.0 74.2 %copy-start.2 = (bf16[288,864]{1,0:T(8,128)(2,1)S(1)}, bf16[288,864]{1,0:T(8,128)(2,1)}, u32[]{:S(2)}) copy-start(bf16[288,864]{1,0:T(8,128)(2,1)} %constant.10.clone.cas_across) | copy-start | bytes 1492996
  2.0 74.3 %copy-start.3 = (f32[128,128]{1,0:T(8,128)S(1)}, f32[128,128]{1,0:T(8,128)}, u32[]{:S(2)}) copy-start(f32[128,128]{1,0:T(8,128)} %constant.11.clone.cas_depth) | copy-start | bytes 196612
  76.2 1.5 %copy-start = (f32[12,288,128]{2,1,0:T(8,128)S(1)}, f32[12,288,128]{2,1,0:T(8,128)}, u32[]{:S(2)}) copy-start(f32[12,288,128]{2,1,0:T(8,128)} %gradient.1.summed) | copy-start | bytes 5308420

commit v2 on v1

--- a/solution.py
+++ b/solution.py
@@ -344,7 +344,7 @@
     at_lane = iota((piece, depth), 1)
     at_row = iota((piece, depth), 0)
     is_first, is_last = at_lane == 0, at_lane == depth - 1
-    spots = iota((piece, columns.shape[1]), 0)
+    spots = iota((width, 2 * columns.shape[1]), 0)
 
     def at(c):
         return pl.ds(c * piece, piece)
@@ -361,113 +361,144 @@
     def behind(value):
         return pltpu.roll(value, 1, 1)
 
+    def ring_sum(held, ends, sides, outer):
+        lanes = jnp.where(is_last, outer, ahead(held)) + jnp.where(is_first, outer, behind(held))
+        return (lanes + ends) + sides
+
     def beside(ref, below, i, above, c, outer):
         held = near(ref, i, c)
-        lanes = jnp.where(is_last, outer, ahead(held)) + jnp.where(is_first, outer, behind(held))
         ends = near(ref, i, c, -1) + near(ref, i, c, 1)
-        return held, (lanes + ends) + (near(ref, below, c) + near(ref, above, c))
+        return held, ring_sum(held, ends, near(ref, below, c) + near(ref, above, c), outer)
+
+    def around_slot(n, base, c):
+        return beside(ring, base + (n - 1) % 4, base + n % 4, base + (n + 1) % 4, c, 0.0)
 
     def partial(value):
         return jnp.sum(value.reshape(piece // 8, 8, depth), axis=0)
 
-    def slot(n, base):
-        return base + lax.rem(n, 4)
-
-    def outside(n):
-        return jnp.logical_or(
-            jnp.logical_and(slab == 0, n < 3), jnp.logical_and(slab == slabs - 1, n >= rows + 3)
-        )
-
-    def prepare(n):
+    def clear(n, store_zero):
+        if n < 3:
+            pl.when(slab == 0)(store_zero)
+        if n >= rows + 3:
+            pl.when(slab == slabs - 1)(store_zero)
+
+    blank_piece = jnp.zeros((piece, depth), F32)
+
+    def prepare(at_row_base, views, n, static):
+        soft_v, _, _, lk_v, wm_v = views
         one = jnp.ones((GUARD, depth), F32)
-        soft[n, 0:GUARD, :] = one
-        soft[n, width + GUARD : width + 2 * GUARD, :] = one
+        soft_v[n, 0:GUARD, :] = one
+        soft_v[n, width + GUARD : width + 2 * GUARD, :] = one
         for c in pieces:
-            value = jnp.exp(0.5 * lk[n, at(c), :].astype(F32))
-            store(soft, n, c, value)
-            store(ring, slot(n, 0), c, value * wm[n, at(c), :].astype(F32))
-
-    def residual(n):
-        spot = columns[...] - (first_row + n - 3) * width
+            value = jnp.exp(0.5 * lk_v[n, at(c), :].astype(F32))
+            store(soft_v, n, c, value)
+            store(ring, n % 4, c, value * wm_v[n, at(c), :].astype(F32))
+
+    def residual(at_row_base, views, n, static):
+        soft_v, res_v = views[:2]
+        spot = spots_at - (first_row + at_row_base + n - 3) * width
+        hits = jnp.where(spots == spot, 1.0, 0.0).astype(BF)
+        source = matmul(hits, sources[...])
         for c in pieces:
-            s, around = beside(soft, n - 1, n, n + 1, c, 1.0)
-            held, total = beside(ring, slot(n - 1, 0), slot(n, 0), slot(n + 1, 0), c, 0.0)
-            hits = jnp.where(spots == spot - c * piece, 1.0, 0.0).astype(BF)
-            value = (s * total - held * around) + matmul(hits, sources[...])
-            res[n, at(c), :] = value
-            store(ring, slot(n, 4), c, s * value)
-            store(ring, slot(n, 12), c, around)
-
-        @pl.when(outside(n))
-        def _():
+            s, around = beside(soft_v, n - 1, n, n + 1, c, 1.0)
+            held, total = around_slot(n, 0, c)
+            value = (s * total - held * around) + source[c * piece : (c + 1) * piece]
+            res_v[n, at(c), :] = value
+            store(ring, 4 + n % 4, c, s * value)
+            store(ring, 12 + n % 4, c, around)
+
+        def store_zero():
             for c in pieces:
-                res[n, at(c), :] = jnp.zeros((piece, depth), F32)
-                store(ring, slot(n, 4), c, jnp.zeros((piece, depth), F32))
-
-    def image(n, own):
+                res_v[n, at(c), :] = blank_piece
+                store(ring, 4 + n % 4, c, blank_piece)
+
+        if static:
+            clear(n, store_zero)
+
+    def image(at_row_base, views, n, static, sums):
+        soft_v, res_v, img_v = views[:3]
         for c in pieces:
-            held, total = beside(ring, slot(n - 1, 4), slot(n, 4), slot(n + 1, 4), c, 0.0)
-            s, value = near(soft, n, c), res[n, at(c), :]
-            applied = held * near(ring, slot(n, 12), c) - s * total
-            img[n, at(c), :] = applied
-            store(ring, slot(n, 8), c, s * applied)
-            acc[0] += own * partial(value * value)
-            acc[1] += own * partial(value * applied)
-
-        @pl.when(outside(n))
-        def _():
+            held, total = around_slot(n, 4, c)
+            s, value = near(soft_v, n, c), res_v[n, at(c), :]
+            applied = held * near(ring, 12 + n % 4, c) - s * total
+            img_v[n, at(c), :] = applied
+            store(ring, 8 + n % 4, c, s * applied)
+            if sums is not None:
+                sums[0].append(partial(value * value))
+                sums[1].append(partial(value * applied))
+
+        def store_zero():
             for c in pieces:
-                img[n, at(c), :] = jnp.zeros((piece, depth), F32)
-                store(ring, slot(n, 8), c, jnp.zeros((piece, depth), F32))
-
-    def twice(n):
+                img_v[n, at(c), :] = blank_piece
+                store(ring, 8 + n % 4, c, blank_piece)
+
+        if static:
+            clear(n, store_zero)
+
+    def twice(at_row_base, views, n, sums):
+        img_v = views[2]
         for c in pieces:
-            held, total = beside(ring, slot(n - 1, 8), slot(n, 8), slot(n + 1, 8), c, 0.0)
-            value = img[n, at(c), :]
-            acc[2] += partial(value * value)
-            acc[3] += partial(held * (value * near(ring, slot(n, 12), c) - total))
-
-    def sweep(first, last, least, most):
-        def step(k, _):
-            if first == 3:
-
-                @pl.when(jnp.logical_and(lax.rem(k - 3, chunk) == 0, k < rows + 3))
-                def _():
-                    for copy in loads((k - 3) // chunk):
-                        copy.wait()
-
-                @pl.when(jnp.logical_and(k == rows + 3, slab < slabs - 1))
-                def _():
-                    for copy in halo(0):
-                        copy.wait_recv()
-
-            prepare(k)
-
-            @pl.when(k >= first + 2)
-            def _():
-                residual(k - 1)
-
-            @pl.when(k >= first + 4)
-            def _():
-                own = jnp.logical_and(k - 2 >= least, k - 2 <= most)
-                image(k - 2, own.astype(F32))
-
-            @pl.when(k >= first + 6)
-            def _():
-                twice(k - 3)
-
-            return 0
-
-        lax.fori_loop(first, last + 1, step, 0)
-
-    sweep(3, rows + 5, 5, rows + 2)
+            held, total = around_slot(n, 8, c)
+            value = img_v[n, at(c), :]
+            sums[2].append(partial(value * value))
+            sums[3].append(partial(held * (value * near(ring, 12 + n % 4, c) - total)))
+
+    def keep(sums):
+        for n, terms in enumerate(sums):
+            if terms:
+                acc[n] += sum(terms[1:], terms[0])
+
+    whole = (soft, res, img, lk, wm)
+
+    def walk(first, last, r_rows, q_rows, q_own, t_rows):
+        sums = [[], [], [], []]
+        for k in range(first, last + 1):
+            if k < rows + 6 and k <= r_rows[1] + 1:
+                prepare(0, whole, k, True)
+            if r_rows[0] <= k - 2 <= r_rows[1]:
+                residual(0, whole, k - 2, True)
+            if q_rows[0] <= k - 4 <= q_rows[1]:
+                own = q_own[0] <= k - 4 <= q_own[1]
+                image(0, whole, k - 4, True, sums if own else None)
+            if t_rows[0] <= k - 5 <= t_rows[1]:
+                twice(0, whole, k - 5, sums)
+        keep(sums)
+
+    def steady(j, _):
+        base = 4 + 4 * j
+        views = [ref.at[pl.ds(base, 11)] for ref in whole]
+        sums = [[], [], [], []]
+        for u in range(4):
+            prepare(base, views, 7 + u, False)
+            residual(base, views, 5 + u, False)
+            image(base, views, 3 + u, False, sums)
+            twice(base, views, 2 + u, sums)
+        keep(sums)
+        return 0
+
+    spots_at = jnp.concatenate([columns[...], columns[...]], axis=1)
+    for copy in loads(0):
+        copy.wait()
+    last = rows + 2
+    walk(3, 10, (4, last + 2), (5, last + 1), (5, last), (6, last))
+    for m in range(1, parts):
+        for copy in loads(m):
+            copy.wait()
+    lax.fori_loop(0, (rows - 8) // 4, steady, 0)
+
+    @pl.when(slab < slabs - 1)
+    def _():
+        for copy in halo(0):
+            copy.wait_recv()
+
+    walk(rows + 3, rows + 8, (4, last + 2), (5, last + 1), (5, last), (6, last))
 
     @pl.when(slab > 0)
     def _():
         for copy in halo(1):
             copy.wait_recv()
 
-    sweep(0, 8, 3, 4)
+    walk(0, 10, (1, 7), (2, 6), (3, 4), (3, 5))
 
     shared[slab] = acc[...]
     copies = [
@@ -825,7 +856,7 @@
         name="gradient",
     )(
         well_columns,
-        jnp.concatenate([obs_columns, obs_columns], axis=1),
+        obs_columns,
         obs_residuals[0],
         log_k,
         warm_adjoint[0],
@@ -866,7 +897,7 @@
 def pick(log_k, heads, warm_adjoint, obs_columns, *rest):
     rows, width, depth = log_k.shape
     count = lax.axis_size("test")
-    fits = depth == 128 and count == 4 and rows % 4 == 0 and rows >= 12 and width % 96 == 0
+    fits = depth == 128 and count == 4 and rows % 4 == 0 and rows >= 16 and width % 96 == 0
     fits = fits and obs_columns.shape[1] % 64 == 0 and rows * width <= 48 * 288
     run = fast if fits and lax.axis_size("space") > 1 else on_device
     return run(log_k, heads, warm_adjoint, obs_columns, *rest)

time: 110 us -> 92 us (0.84)
  Pallas kernels: 105 us -> 88.4 us
  other arithmetic: 1.31 us -> 0 us
    pallas_call x1, Pallas kernels: 74.2 us -> 58.2 us  [fast(): pl.pallas_call(gradient_kernel, out_shape=shape(groups, width, depth), in...]
    concatenate x1 -> x0, other arithmetic: 1.31 us -> none  [fast(): jnp.concatenate([obs_columns, obs_columns], axis=1)]
where the time goes in v2:
time: 92 us; the launch traced here: 91.8 us
  Pallas kernels  88.4 us (96%)
  local copies, waits for them, and re-layouts  2.7 us (3%)
    pallas_call x1, Pallas kernels, fast(): pl.pallas_call(gradient_kernel, out_shape=shape(groups, width, depth), in...  58.2 us
    pallas_call x1, Pallas kernels, fast(): pl.pallas_call(spectral_kernel, out_shape=shape(rows, part, depth), in_sp...  30.2 us
    unnamed x9, local copies, waits for them, and re-layouts  2.7 us

profile of v2, /device:TPU:0, one launch (start us, length us, event | category | flops | bytes accessed | tf_op | source)
XLA Modules:
  0.0 91.8 jit_solution(13012158322943999272)
XLA Ops:
  0.7 0.0 copy-start.1
  0.7 0.0 copy-start.2
  0.7 0.0 copy-start.3
  0.7 58.2 %gradient.1.summed = f32[12,288,128]{2,1,0:T(8,128)} custom-call(s32[1]{0:T(128)S(6)} %copy.12.well, s32[1,64]{1,0:T(1,128)} %columns.1, f32[64,128]{1,0:T(8,128)} %bitcast.5, bf16[48,288,128]{2,1,0:T(8,128)(2,1)} %logk.1, bf16[48,288,128]{2,1,0:T(8,128)(2,1)} %bitcast.3, bf16[48,288,128]{2,1,0:T(8,128)(2,1)} %bitcast.4, ...), custom_call_target="tpu_custom_call" | custom-call | tf_op jit(solution)/shard_map/gradient/pallas_call | solution.py:830
  58.9 0.0 copy-done.1
  58.9 0.0 copy-done.2
  58.9 0.0 copy-done.3
  58.9 0.0 copy-start
  59.0 1.5 %copy-done = f32[12,288,128]{2,1,0:T(8,128)S(1)} copy-done((f32[12,288,128]{2,1,0:T(8,128)S(1)}, f32[12,288,128]{2,1,0:T(8,128)}, u32[]{:S(2)}) %copy-start) | copy-done | bytes 1769496
  60.4 30.2 %spectral.1 = f32[48,72,128]{2,1,0:T(8,128)S(1)} custom-call(f32[12,288,128]{2,1,0:T(8,128)S(1)} %copy-done, f32[4,6,72,128]{3,2,1,0:T(8,128)S(1)} %copy-done.1, bf16[288,864]{1,0:T(8,128)(2,1)S(1)} %copy-done.2, f32[128,128]{1,0:T(8,128)S(1)} %copy-done.3), custom_call_target="tpu_custom_call" | custom-call | tf_op jit(solution)/shard_map/spectral/pallas_call | solution.py:867
  90.6 1.2 %copy.13 = f32[48,72,128]{2,1,0:T(8,128)} copy(f32[48,72,128]{2,1,0:T(8,128)S(1)} %spectral.1) | data formatting | bytes 3538944
Async XLA Ops:
  0.7 58.3 %copy-start.1 = (f32[4,6,72,128]{3,2,1,0:T(8,128)S(1)}, f32[4,6,72,128]{3,2,1,0:T(8,128)}, u32[]{:S(2)}) copy-start(f32[4,6,72,128]{3,2,1,0:T(8,128)} %constant.9.clone.listed) | copy-start | bytes 2654212
  0.7 58.3 %copy-start.2 = (bf16[288,864]{1,0:T(8,128)(2,1)S(1)}, bf16[288,864]{1,0:T(8,128)(2,1)}, u32[]{:S(2)}) copy-start(bf16[288,864]{1,0:T(8,128)(2,1)} %constant.10.clone.cas_across) | copy-start | bytes 1492996
  0.7 58.3 %copy-start.3 = (f32[128,128]{1,0:T(8,128)S(1)}, f32[128,128]{1,0:T(8,128)}, u32[]{:S(2)}) copy-start(f32[128,128]{1,0:T(8,128)} %constant.11.clone.cas_depth) | copy-start | bytes 196612
  58.9 1.5 %copy-start = (f32[12,288,128]{2,1,0:T(8,128)S(1)}, f32[12,288,128]{2,1,0:T(8,128)}, u32[]{:S(2)}) copy-start(f32[12,288,128]{2,1,0:T(8,128)} %gradient.1.summed) | copy-start | bytes 5308420

commit v3 on v2

--- a/solution.py
+++ b/solution.py
@@ -231,7 +231,7 @@
     pl.semaphore_wait(barrier, len(others))
 
 
-def gradient_kernel(
+def whole_kernel(
     well,
     columns,
     observed,
@@ -239,6 +239,9 @@
     warm,
     heads,
     turned,
+    listed,
+    cas_across,
+    cas_depth,
     out,
     lk,
     wm,
@@ -263,6 +266,16 @@
     take_mate,
     send_across,
     take_across,
+    tables,
+    freq,
+    moments,
+    going,
+    coming,
+    table_sem,
+    send_end,
+    take_end,
+    send_back,
+    take_back,
 ):
     rows, width, depth = logk.shape
     parts = 4
@@ -307,7 +320,11 @@
             )
         return copies
 
-    greet(others + [mate, across])
+    count = 4
+    peers = [lax.rem(here + k, count) for k in range(1, count)]
+    fetch = pltpu.make_async_copy(listed.at[here], tables, table_sem)
+    fetch.start()
+    greet(others + [{"test": peer} for peer in peers])
 
     @pl.when(slab > 0)
     def _():
@@ -555,7 +572,6 @@
 
     fill(2)
     fill(3)
-    count = 4
     groups = rows // count
     at_block = at_lane // (depth // count)
 
@@ -591,7 +607,6 @@
                 for b in range(1, count):
                     joined = jnp.where(at_block == b, turns[(b - t) % count], joined)
                 mine[t % 2, g, t // 2, at(c), :] = joined
-        to_mate(g).start()
 
     def to_mate(g):
         return pltpu.make_async_remote_copy(
@@ -618,70 +633,57 @@
         ship[g] = encode(mine[core, g, 1 - half] + from_mate[g, 1 - half], 16)
         to_across(g).start()
 
-    group(0)
-
-    def step(g, _):
-        group(g)
-        relay(g - 1)
-        return 0
-
-    lax.fori_loop(1, groups, step, 0)
-    relay(groups - 1)
-
-    def finish(g, _):
+    part = width // count
+    spare = going.shape[2] - part
+    lanes = depth
+    turn = lax.rem((count - here) * (lanes // count), lanes)
+    filtered = res.at[:, pl.ds(0, part)]
+
+    def settle(g):
         to_across(g).wait_recv()
-        out[g] = (mine[core, g, half] + from_mate[g, half]) + decode(got[g], 16)
         to_mate(g).wait_send()
         to_across(g).wait_send()
-        return 0
-
-    lax.fori_loop(0, groups, finish, 0)
-
-
-def spectral_kernel(
-    summed,
-    listed,
-    cas_across,
-    cas_depth,
-    out,
-    tables,
-    freq,
-    moments,
-    filtered,
-    going,
-    coming,
-    load_sem,
-    send_end,
-    take_end,
-    send_back,
-    take_back,
-):
-    groups, width, lanes = summed.shape
-    count, part = going.shape[0], width // going.shape[0]
-    spare = going.shape[2] - part
-    rows = groups * count
-    slabs = moments.shape[0]
-    slab, here = lax.axis_index("space"), lax.axis_index("test")
-    others = [{"space": lax.rem(slab + k, slabs)} for k in range(1, slabs)]
-    peers = [lax.rem(here + k, count) for k in range(1, count)]
-    fetch = pltpu.make_async_copy(listed.at[here], tables, load_sem)
-    fetch.start()
-    greet(others + [{"test": peer} for peer in peers])
-    turn = lax.rem((count - here) * (lanes // count), lanes)
-
-    def mix(g, _):
-        top, low = halves(pltpu.roll(summed[g], turn, 1))
+
+    def absorb(g):
+        summed = (mine[core, g, half] + from_mate[g, half]) + decode(got[g], 16)
+        top, low = halves(pltpu.roll(summed, turn, 1))
         mixed = matmul(cas_across[...], jnp.concatenate([top, top, low], axis=0))
         blocks = [mixed[j * part : (j + 1) * part] for j in range(count)]
         for p, plane in enumerate(swap_blocks(blocks)):
             freq[g * count + p] = plane
+
+    lag = 4
+
+    def early(g, _):
+        group(g)
+        to_mate(g).start()
+        relay(g - 1)
         return 0
 
-    lax.fori_loop(0, groups, mix, 0)
+    def late(g, _):
+        settle(g - lag)
+        absorb(g - lag)
+        group(g)
+        to_mate(g).start()
+        relay(g - 1)
+        return 0
+
+    group(0)
+    to_mate(0).start()
+    lax.fori_loop(1, lag, early, 0)
+    lax.fori_loop(lag, groups, late, 0)
+    relay(groups - 1)
+
+    def finish(g, _):
+        settle(g)
+        absorb(g)
+        return 0
+
+    lax.fori_loop(groups - lag, groups, finish, 0)
     fetch.wait()
     pole, level, slope, decay, wrap_one, wrap_two = (tables[n] for n in range(6))
 
-    def walk(i, carry):
+    def gather(i, carry):
         one, two, back_one, back_two = carry
         value, back = freq[i], freq[rows - 1 - i]
         return (
@@ -692,7 +694,7 @@
         )
 
     zero = jnp.zeros((part, lanes), jnp.float32)
-    ends = lax.fori_loop(0, rows, walk, (zero, zero, zero, zero))
+    ends = lax.fori_loop(0, rows, gather, (zero, zero, zero, zero))
     for n in range(4):
         moments[slab, n] = encode(ends[n], spare)
     copies = [
@@ -750,28 +752,34 @@
             device_id_type=MESH,
         )
 
-    def unmix(g, _):
-        blocks = swap_blocks([filtered[g * count + p] for p in range(count)])
-        top, low = halves(jnp.concatenate(blocks, axis=0))
-        mixed = matmul(cas_across[...], jnp.concatenate([top, top, low], axis=0))
-        for u in range(count):
-            going[u, g] = encode(mixed[u * part : (u + 1) * part], spare)
-        for k in range(count - 1):
-            to_peer(k, g).start()
-        coming[here, g] = going[here, g]
+    pair = 2
+
+    def unmix(j, _):
+        for g in [pair * j + n for n in range(pair)]:
+            blocks = swap_blocks([filtered[g * count + p] for p in range(count)])
+            top, low = halves(jnp.concatenate(blocks, axis=0))
+            mixed = matmul(cas_across[...], jnp.concatenate([top, top, low], axis=0))
+            for u in range(count):
+                going[u, g] = encode(mixed[u * part : (u + 1) * part], spare)
+        for g in [pair * j + n for n in range(pair)]:
+            for k in range(count - 1):
+                to_peer(k, g).start()
+            coming[here, g] = going[here, g]
         return 0
 
-    lax.fori_loop(0, groups, unmix, 0)
-
-    def back(g, _):
-        for k in range(count - 1):
-            to_peer(k, g).wait()
-        planes = [decode(coming[t, g], spare) for t in range(count)]
-        for p, plane in enumerate(swap_blocks(planes)):
-            out[g * count + p] = dot3(plane, cas_depth[...])
+    lax.fori_loop(0, groups // pair, unmix, 0)
+
+    def back(j, _):
+        for g in [pair * j + n for n in range(pair)]:
+            for k in range(count - 1):
+                to_peer(k, g).wait()
+        for g in [pair * j + n for n in range(pair)]:
+            planes = [decode(coming[t, g], spare) for t in range(count)]
+            for p, plane in enumerate(swap_blocks(planes)):
+                out[g * count + p] = dot3(plane, cas_depth[...])
         return 0
 
-    lax.fori_loop(0, groups, back, 0)
+    lax.fori_loop(0, groups // pair, back, 0)
 
 
 def table(length):
@@ -827,10 +835,11 @@
     planes = rows + 6
     padded = width + 2 * GUARD
     spare = 16 - part % 16
-    summed = pl.pallas_call(
-        gradient_kernel,
-        out_shape=shape(groups, width, depth),
-        in_specs=[SM, VM, VM, ANY, ANY, ANY, VM],
+    top, low = split(table(width))
+    return pl.pallas_call(
+        whole_kernel,
+        out_shape=shape(rows, part, depth),
+        in_specs=[SM, VM, VM, ANY, ANY, ANY, VM, ANY, VM, VM],
         out_specs=VM,
         scratch_shapes=[pltpu.VMEM((planes, width, depth), BF)] * 3
         + [
@@ -849,11 +858,21 @@
         ]
         + [pltpu.SemaphoreType.DMA((2, 3))] * 2
         + [pltpu.SemaphoreType.DMA((slabs - 1,))] * 2
-        + [pltpu.SemaphoreType.DMA((groups,))] * 4,
+        + [pltpu.SemaphoreType.DMA((groups,))] * 4
+        + [
+            pltpu.VMEM((6, part, depth), F32),
+            pltpu.VMEM((rows, part, depth), F32),
+            pltpu.VMEM((slabs, 4, part + spare, depth), jnp.int16),
+            pltpu.VMEM((count, groups, part + spare, depth), jnp.int16),
+            pltpu.VMEM((count, groups, part + spare, depth), jnp.int16),
+            pltpu.SemaphoreType.DMA,
+        ]
+        + [pltpu.SemaphoreType.DMA((slabs - 1,))] * 2
+        + [pltpu.SemaphoreType.DMA((count - 1, groups))] * 2,
         compiler_params=pltpu.CompilerParams(
-            vmem_limit_bytes=60 * 1024 * 1024, collective_id=1, has_side_effects=True
+            vmem_limit_bytes=63 * 1024 * 1024, collective_id=1, has_side_effects=True
         ),
-        name="gradient",
+        name="whole",
     )(
         well_columns,
         obs_columns,
@@ -862,32 +881,6 @@
         warm_adjoint[0],
         heads[0],
         jnp.asarray(turned_tables(depth, count)),
-    )
-    top, low = split(table(width))
-    return pl.pallas_call(
-        spectral_kernel,
-        out_shape=shape(rows, part, depth),
-        in_specs=[VM, ANY, VM, VM],
-        out_specs=VM,
-        scratch_shapes=[
-            pltpu.VMEM((6, part, depth), F32),
-            pltpu.VMEM((rows, part, depth), F32),
-            pltpu.VMEM((slabs, 4, part + spare, depth), jnp.int16),
-            pltpu.VMEM((rows, part, depth), F32),
-            pltpu.VMEM((count, groups, part + spare, depth), jnp.int16),
-            pltpu.VMEM((count, groups, part + spare, depth), jnp.int16),
-            pltpu.SemaphoreType.DMA,
-            pltpu.SemaphoreType.DMA((slabs - 1,)),
-            pltpu.SemaphoreType.DMA((slabs - 1,)),
-            pltpu.SemaphoreType.DMA((count - 1, groups)),
-            pltpu.SemaphoreType.DMA((count - 1, groups)),
-        ],
-        compiler_params=pltpu.CompilerParams(
-            vmem_limit_bytes=40 * 1024 * 1024, collective_id=2, has_side_effects=True
-        ),
-        name="spectral",
-    )(
-        summed,
         jnp.asarray(filter_tables(rows, rows * slabs, width, depth, count)),
         jnp.asarray(np.concatenate([top, low, top], axis=1)),
         jnp.asarray(table(depth)),
@@ -897,7 +890,7 @@
 def pick(log_k, heads, warm_adjoint, obs_columns, *rest):
     rows, width, depth = log_k.shape
     count = lax.axis_size("test")
-    fits = depth == 128 and count == 4 and rows % 4 == 0 and rows >= 16 and width % 96 == 0
+    fits = depth == 128 and count == 4 and rows % 8 == 0 and rows >= 16 and width % 96 == 0
     fits = fits and obs_columns.shape[1] % 64 == 0 and rows * width <= 48 * 288
     run = fast if fits and lax.axis_size("space") > 1 else on_device
     return run(log_k, heads, warm_adjoint, obs_columns, *rest)

time: 92 us -> 87.1 us (0.947)
  Pallas kernels: 88.4 us -> 83.4 us
    pallas_call x2 -> x1, Pallas kernels: 88.4 us -> 83.4 us  [fast(): pl.pallas_call(whole_kernel, out_shape=shape(rows, part, depth), in_specs...]
    unnamed x9 -> x1, local copies, waits for them, and re-layouts: 2.7 us -> 2.8 us
where the time goes in v3:
time: 87.1 us; the launch traced here: 86.9 us
  Pallas kernels  83.4 us (96%)
  local copies, waits for them, and re-layouts  2.8 us (3%)
    pallas_call x1, Pallas kernels, fast(): pl.pallas_call(whole_kernel, out_shape=shape(rows, part, depth), in_specs...  83.4 us
    unnamed x1, local copies, waits for them, and re-layouts  2.8 us

profile of v3, /device:TPU:0, one launch (start us, length us, event | category | flops | bytes accessed | tf_op | source)
XLA Modules:
  0.0 86.9 jit_solution(4177659869782088588)
XLA Ops:
  0.7 83.4 %whole.1 = f32[48,72,128]{2,1,0:T(8,128)} custom-call(s32[1]{0:T(128)S(6)} %copy.12.well, s32[1,64]{1,0:T(1,128)} %columns.1, f32[64,128]{1,0:T(8,128)} %bitcast.5, bf16[48,288,128]{2,1,0:T(8,128)(2,1)} %logk.1, bf16[48,288,128]{2,1,0:T(8,128)(2,1)} %bitcast.3, bf16[48,288,128]{2,1,0:T(8,128)(2,1)} %bitcast.4, bf16[4,256,256]{2,1,0:T(8,128)(2,1)} %constant.8.clone.turned, ...), custom_call_target="tpu_custom_call" | custom-call | tf_op jit(solution)/shard_map/whole/pallas_call | solution.py:839
  84.1 2.8 %copy.13 = f32[48,72,128]{2,1,0:T(8,128)} copy(f32[48,72,128]{2,1,0:T(8,128)} %whole.1) | data formatting | bytes 3538944

commit v4 on v3

--- a/solution.py
+++ b/solution.py
@@ -159,8 +159,10 @@
 
 
 GUARD = 8
+RING = 6
 STEP = 256.0
 TOP = 32000.0
+HALF_LOG = 0.5 / float(np.log(2.0))
 BF = jnp.bfloat16
 F32 = jnp.float32
 VM = pl.BlockSpec(memory_space=pltpu.VMEM)
@@ -184,12 +186,6 @@
 
 def matmul(a, b):
     return jnp.dot(a, b, preferred_element_type=F32)
-
-
-def dot3(a, b):
-    a_top, a_low = halves(a)
-    b_top, b_low = halves(b)
-    return matmul(a_top, b_top) + (matmul(a_top, b_low) + matmul(a_low, b_top))
 
 
 def encode(values, spare):
@@ -209,19 +205,23 @@
 
 
 def swap_blocks(planes):
+    planes = list(planes)
     count = len(planes)
     lanes = planes[0].shape[1]
     block = lanes // count
-    at_lane = iota(planes[0].shape, 1) // block
-    swapped = []
-    for to in range(count):
-        joined = planes[to]
-        for frm in range(count):
-            if frm != to:
-                shift = (block * (frm - to)) % lanes
-                joined = jnp.where(at_lane == frm, pltpu.roll(planes[frm], shift, 1), joined)
-        swapped.append(joined)
-    return swapped
+    at_block = iota(planes[0].shape, 1) // block
+    span = 1
+    while span < count:
+        odd = (at_block // span) % 2 == 1
+        for low in range(count):
+            if (low // span) % 2 == 0:
+                first, second = planes[low], planes[low + span]
+                up = pltpu.roll(second, block * span, 1)
+                down = pltpu.roll(first, lanes - block * span, 1)
+                planes[low] = jnp.where(odd, up, first)
+                planes[low + span] = jnp.where(odd, second, down)
+        span *= 2
+    return planes
 
 
 def greet(others):
@@ -239,13 +239,14 @@
     warm,
     heads,
     turned,
+    beside_lanes,
     listed,
     cas_across,
     cas_depth,
     out,
     lk,
     wm,
-    hd,
+    level_ends,
     soft,
     res,
     img,
@@ -295,7 +296,7 @@
         to = pl.ds(3 + m * chunk, chunk)
         return [
             pltpu.make_async_copy(frm.at[span], held.at[to], load_sem.at[n, m])
-            for n, (frm, held) in enumerate(((logk, lk), (warm, wm), (heads, hd)))
+            for n, (frm, held) in enumerate(((logk, lk), (warm, wm)))
         ]
 
     for m in range(parts):
@@ -305,9 +306,11 @@
     def halo(direction):
         up = direction == 1
         copies = []
-        for n, (frm, held, deep) in enumerate(((logk, lk, 3), (warm, wm, 3), (heads, hd, 1))):
+        for n, (frm, held, deep) in enumerate(((logk, lk, 3), (warm, wm, 3), (heads, level_ends, 1))):
             at = rows - deep if up else 0
             to = 3 - deep if up else 3 + rows
+            if deep == 1:
+                to = 0 if up else 1
             copies.append(
                 pltpu.make_async_remote_copy(
                     src_ref=frm.at[pl.ds(at, deep)],
@@ -342,13 +345,13 @@
     def _():
         lk[0:3] = blank
         wm[0:3] = blank
-        hd[0:3] = blank
+        level_ends[0] = blank[0]
 
     @pl.when(slab == slabs - 1)
     def _():
         lk[rows + 3 : rows + 6] = blank
         wm[rows + 3 : rows + 6] = blank
-        hd[rows + 3 : rows + 6] = blank
+        level_ends[1] = blank[0]
 
     top, low = halves(observed[...])
     sources[...] = jnp.concatenate([top, low], axis=0)
@@ -407,7 +410,7 @@
         soft_v[n, 0:GUARD, :] = one
         soft_v[n, width + GUARD : width + 2 * GUARD, :] = one
         for c in pieces:
-            value = jnp.exp(0.5 * lk_v[n, at(c), :].astype(F32))
+            value = jnp.exp2(HALF_LOG * lk_v[n, at(c), :].astype(F32))
             store(soft_v, n, c, value)
             store(ring, n % 4, c, value * wm_v[n, at(c), :].astype(F32))
 
@@ -434,8 +437,13 @@
 
     def image(at_row_base, views, n, static, sums):
         soft_v, res_v, img_v = views[:3]
+        plane = ring[4 + n % 4, pl.ds(GUARD, width), :]
+        lanes = matmul(jnp.concatenate(halves(plane), axis=1), beside_lanes[...])
         for c in pieces:
-            held, total = around_slot(n, 4, c)
+            held = near(ring, 4 + n % 4, c)
+            ends = near(ring, 4 + n % 4, c, -1) + near(ring, 4 + n % 4, c, 1)
+            sides = near(ring, 4 + (n - 1) % 4, c) + near(ring, 4 + (n + 1) % 4, c)
+            total = (lanes[c * piece : (c + 1) * piece] + ends) + sides
             s, value = near(soft_v, n, c), res_v[n, at(c), :]
             applied = held * near(ring, 12 + n % 4, c) - s * total
             img_v[n, at(c), :] = applied
@@ -455,10 +463,11 @@
     def twice(at_row_base, views, n, sums):
         img_v = views[2]
         for c in pieces:
-            held, total = around_slot(n, 8, c)
-            value = img_v[n, at(c), :]
+            held, value = near(ring, 8 + n % 4, c), img_v[n, at(c), :]
+            after = near(ring, 8 + (n + 1) % 4, c) + near(ring, 8 + n % 4, c, 1)
+            after = after + jnp.where(is_last, 0.0, ahead(held))
             sums[2].append(partial(value * value))
-            sums[3].append(partial(held * (value * near(ring, 12 + n % 4, c) - total)))
+            sums[3].append(partial(held * (value * near(ring, 12 + n % 4, c) - 2.0 * after)))
 
     def keep(sums):
         for n, terms in enumerate(sums):
@@ -517,6 +526,10 @@
 
     walk(0, 10, (1, 7), (2, 6), (3, 4), (3, 5))
 
+    levels_in = pltpu.make_async_copy(heads, lk.at[pl.ds(3, rows)], load_sem.at[0, 0])
+    levels_in.start()
+    lk[2] = level_ends[0]
+    lk[rows + 3] = level_ends[1]
     shared[slab] = acc[...]
     copies = [
         pltpu.make_async_remote_copy(
@@ -544,6 +557,7 @@
 
     for copy in copies:
         copy.wait()
+    levels_in.wait()
 
     def gathered(n):
         total = shared[0, n]
@@ -568,12 +582,15 @@
             field = wm[n, at(c), :].astype(F32)
             field = field + (with_start * res[n, at(c), :] - with_image * img[n, at(c), :])
             store(ring, eighth(n, 0), c, field)
-            store(ring, eighth(n, 8), c, hd[n, at(c), :].astype(F32))
+            store(ring, eighth(n, 8), c, lk[n, at(c), :].astype(F32))
 
     fill(2)
     fill(3)
     groups = rows // count
     at_block = at_lane // (depth // count)
+
+    def turn(g):
+        return lax.rem(g, RING)
 
     def group(g):
         start = 3 + count * g
@@ -606,11 +623,11 @@
                 joined = turns[-t % count]
                 for b in range(1, count):
                     joined = jnp.where(at_block == b, turns[(b - t) % count], joined)
-                mine[t % 2, g, t // 2, at(c), :] = joined
+                mine[t % 2, turn(g), t // 2, at(c), :] = joined
 
     def to_mate(g):
         return pltpu.make_async_remote_copy(
-            src_ref=mine.at[1 - core, g],
+            src_ref=mine.at[1 - core, turn(g)],
             dst_ref=from_mate.at[g],
             send_sem=send_mate.at[g],
             recv_sem=take_mate.at[g],
@@ -620,7 +637,7 @@
 
     def to_across(g):
         return pltpu.make_async_remote_copy(
-            src_ref=ship.at[g],
+            src_ref=ship.at[turn(g)],
             dst_ref=got.at[g],
             send_sem=send_across.at[g],
             recv_sem=take_across.at[g],
@@ -630,13 +647,12 @@
 
     def relay(g):
         to_mate(g).wait_recv()
-        ship[g] = encode(mine[core, g, 1 - half] + from_mate[g, 1 - half], 16)
+        ship[turn(g)] = encode(mine[core, turn(g), 1 - half] + from_mate[g, 1 - half], 16)
         to_across(g).start()
 
     part = width // count
     spare = going.shape[2] - part
     lanes = depth
-    turn = lax.rem((count - here) * (lanes // count), lanes)
     filtered = res.at[:, pl.ds(0, part)]
 
     def settle(g):
@@ -645,12 +661,12 @@
         to_across(g).wait_send()
 
     def absorb(g):
-        summed = (mine[core, g, half] + from_mate[g, half]) + decode(got[g], 16)
-        top, low = halves(pltpu.roll(summed, turn, 1))
+        summed = (mine[core, turn(g), half] + from_mate[g, half]) + decode(got[g], 16)
+        top, low = halves(summed)
         mixed = matmul(cas_across[...], jnp.concatenate([top, top, low], axis=0))
         blocks = [mixed[j * part : (j + 1) * part] for j in range(count)]
         for p, plane in enumerate(swap_blocks(blocks)):
-            freq[g * count + p] = plane
+            freq[g * count + lax.rem(p - here + count, count)] = plane
 
     lag = 4
 
@@ -755,12 +771,16 @@
     pair = 2
 
     def unmix(j, _):
+        both = []
         for g in [pair * j + n for n in range(pair)]:
             blocks = swap_blocks([filtered[g * count + p] for p in range(count)])
             top, low = halves(jnp.concatenate(blocks, axis=0))
-            mixed = matmul(cas_across[...], jnp.concatenate([top, top, low], axis=0))
+            both.append(jnp.concatenate([top, top, low], axis=0))
+        mixed = matmul(cas_across[...], jnp.concatenate(both, axis=1))
+        for n in range(pair):
             for u in range(count):
-                going[u, g] = encode(mixed[u * part : (u + 1) * part], spare)
+                block = mixed[u * part : (u + 1) * part, n * lanes : (n + 1) * lanes]
+                going[u, pair * j + n] = encode(block, spare)
         for g in [pair * j + n for n in range(pair)]:
             for k in range(count - 1):
                 to_peer(k, g).start()
@@ -776,7 +796,8 @@
         for g in [pair * j + n for n in range(pair)]:
             planes = [decode(coming[t, g], spare) for t in range(count)]
             for p, plane in enumerate(swap_blocks(planes)):
-                out[g * count + p] = dot3(plane, cas_depth[...])
+                double = matmul(jnp.concatenate(halves(plane), axis=1), cas_depth[...])
+                out[g * count + p] = double[:, :lanes] + double[:, lanes:]
         return 0
 
     lax.fori_loop(0, groups // pair, back, 0)
@@ -793,11 +814,15 @@
     return top, (values - top.astype(np.float32)).astype(jnp.bfloat16)
 
 
+def doubled_table(values):
+    top, low = split(values)
+    return np.block([[top, low], [top, np.zeros_like(low)]])
+
+
 def turned_tables(length, count):
     tables = []
     for p in range(count):
-        top, low = split(-0.5 * np.roll(table(length), p * (length // count), axis=1))
-        tables.append(np.block([[top, low], [top, np.zeros_like(low)]]))
+        tables.append(doubled_table(-0.5 * np.roll(table(length), p * (length // count), axis=1)))
     return np.stack(tables)
 
 
@@ -839,10 +864,11 @@
     return pl.pallas_call(
         whole_kernel,
         out_shape=shape(rows, part, depth),
-        in_specs=[SM, VM, VM, ANY, ANY, ANY, VM, ANY, VM, VM],
+        in_specs=[SM, VM, VM, ANY, ANY, ANY, VM, VM, ANY, VM, VM],
         out_specs=VM,
-        scratch_shapes=[pltpu.VMEM((planes, width, depth), BF)] * 3
+        scratch_shapes=[pltpu.VMEM((planes, width, depth), BF)] * 2
         + [
+            pltpu.VMEM((2, width, depth), BF),
             pltpu.VMEM((planes, padded, depth), F32),
             pltpu.VMEM((planes, width, depth), F32),
             pltpu.VMEM((planes, width, depth), F32),
@@ -850,11 +876,11 @@
             pltpu.VMEM((2 * observed, depth), BF),
             pltpu.VMEM((4, 8, depth), F32),
             pltpu.VMEM((slabs, 4, 8, depth), F32),
-            pltpu.VMEM((2, groups, 2, width, depth), F32),
+            pltpu.VMEM((2, RING, 2, width, depth), F32),
             pltpu.VMEM((groups, 2, width, depth), F32),
+            pltpu.VMEM((RING, width + 16, depth), jnp.int16),
             pltpu.VMEM((groups, width + 16, depth), jnp.int16),
-            pltpu.VMEM((groups, width + 16, depth), jnp.int16),
-            pltpu.SemaphoreType.DMA((3, 4)),
+            pltpu.SemaphoreType.DMA((2, 4)),
         ]
         + [pltpu.SemaphoreType.DMA((2, 3))] * 2
         + [pltpu.SemaphoreType.DMA((slabs - 1,))] * 2
@@ -870,7 +896,7 @@
         + [pltpu.SemaphoreType.DMA((slabs - 1,))] * 2
         + [pltpu.SemaphoreType.DMA((count - 1, groups))] * 2,
         compiler_params=pltpu.CompilerParams(
-            vmem_limit_bytes=63 * 1024 * 1024, collective_id=1, has_side_effects=True
+            vmem_limit_bytes=60 * 1024 * 1024, collective_id=1, has_side_effects=True
         ),
         name="whole",
     )(
@@ -881,9 +907,10 @@
         warm_adjoint[0],
         heads[0],
         jnp.asarray(turned_tables(depth, count)),
+        jnp.asarray(np.tile(np.eye(depth, k=1) + np.eye(depth, k=-1), (2, 1)), BF),
         jnp.asarray(filter_tables(rows, rows * slabs, width, depth, count)),
         jnp.asarray(np.concatenate([top, low, top], axis=1)),
-        jnp.asarray(table(depth)),
+        jnp.asarray(doubled_table(table(depth))),
     )
 
 

time: 87.1 us -> 81.9 us (0.940)
  Pallas kernels: 83.4 us -> 78.2 us
    pallas_call x1, Pallas kernels: 83.4 us -> 78.2 us  [fast(): pl.pallas_call(whole_kernel, out_shape=shape(rows, part, depth), in_specs...]
where the time goes in v4:
time: 81.9 us; the launch traced here: 81.6 us
  Pallas kernels  78.2 us (95%)
  local copies, waits for them, and re-layouts  2.8 us (3%)
    pallas_call x1, Pallas kernels, fast(): pl.pallas_call(whole_kernel, out_shape=shape(rows, part, depth), in_specs...  78.2 us
    unnamed x1, local copies, waits for them, and re-layouts  2.8 us

profile of v4, /device:TPU:0, one launch (start us, length us, event | category | flops | bytes accessed | tf_op | source)
XLA Modules:
  0.0 81.6 jit_solution(16133573392671476346)
XLA Ops:
  0.7 78.2 %whole.1 = f32[48,72,128]{2,1,0:T(8,128)} custom-call(s32[1]{0:T(128)S(6)} %copy.13.well, s32[1,64]{1,0:T(1,128)} %columns.1, f32[64,128]{1,0:T(8,128)} %bitcast.5, bf16[48,288,128]{2,1,0:T(8,128)(2,1)} %logk.1, bf16[48,288,128]{2,1,0:T(8,128)(2,1)} %bitcast.3, bf16[48,288,128]{2,1,0:T(8,128)(2,1)} %bitcast.4, bf16[4,256,256]{2,1,0:T(8,128)(2,1)} %constant.10.clone.turned, ...), custom_call_target="tpu_custom_call" | custom-call | tf_op jit(solution)/shard_map/whole/pallas_call | solution.py:864
  78.8 2.8 %copy.14 = f32[48,72,128]{2,1,0:T(8,128)} copy(f32[48,72,128]{2,1,0:T(8,128)} %whole.1) | data formatting | bytes 3538944

commit v5 on v4

--- a/solution.py
+++ b/solution.py
@@ -277,6 +277,7 @@
     take_end,
     send_back,
     take_back,
+    ends,
 ):
     rows, width, depth = logk.shape
     parts = 4
@@ -530,7 +531,8 @@
     levels_in.start()
     lk[2] = level_ends[0]
     lk[rows + 3] = level_ends[1]
-    shared[slab] = acc[...]
+    rows_of = [jnp.sum(acc[n], axis=0, keepdims=True) for n in range(4)]
+    shared[slab] = jnp.concatenate(rows_of + [jnp.zeros((4, depth), F32)], axis=0)
     copies = [
         pltpu.make_async_remote_copy(
             src_ref=shared.at[slab],
@@ -558,12 +560,15 @@
     for copy in copies:
         copy.wait()
     levels_in.wait()
+    fetch.wait()
+
+    collected = shared[0]
+    for m in range(1, slabs):
+        collected = collected + shared[m]
 
     def gathered(n):
-        total = shared[0, n]
-        for m in range(1, slabs):
-            total = total + shared[m, n]
-        return jnp.broadcast_to(jnp.sum(total, axis=(0, 1), keepdims=True), (1, depth))
+        total = jnp.sum(collected[n : n + 1], axis=1, keepdims=True)
+        return jnp.broadcast_to(total, (1, depth))
 
     norm, curve, square, bend = [gathered(n) for n in range(4)]
     length = norm / curve
@@ -667,7 +672,20 @@
         blocks = [mixed[j * part : (j + 1) * part] for j in range(count)]
         for p, plane in enumerate(swap_blocks(blocks)):
             freq[g * count + lax.rem(p - here + count, count)] = plane
-
+        pole = tables[0]
+        one, two, back_one, back_two, power = (ends[n] for n in range(5))
+        for p in range(count):
+            value = freq[g * count + p]
+            one, two = value + pole * one, pole * (two + one)
+            weighted = value * power
+            back_one = back_one + weighted
+            back_two = back_two + (g * count + p).astype(F32) * weighted
+            power = power * pole
+        for n, value in enumerate((one, two, back_one, back_two, power)):
+            ends[n] = value
+
+    ends[0:4] = jnp.zeros((4, part, lanes), F32)
+    ends[4] = jnp.ones((part, lanes), F32)
     lag = 4
 
     def early(g, _):
@@ -696,37 +714,29 @@
         return 0
 
     lax.fori_loop(groups - lag, groups, finish, 0)
-    fetch.wait()
     pole, level, slope, decay, wrap_one, wrap_two = (tables[n] for n in range(6))
-
-    def gather(i, carry):
-        one, two, back_one, back_two = carry
-        value, back = freq[i], freq[rows - 1 - i]
-        return (
-            value + pole * one,
-            pole * (two + one),
-            back + pole * back_one,
-            pole * (back_two + back_one),
-        )
-
-    zero = jnp.zeros((part, lanes), jnp.float32)
-    ends = lax.fori_loop(0, rows, gather, (zero, zero, zero, zero))
-    for n in range(4):
-        moments[slab, n] = encode(ends[n], spare)
-    copies = [
-        pltpu.make_async_remote_copy(
-            src_ref=moments.at[slab],
-            dst_ref=moments.at[slab],
-            send_sem=send_end.at[k],
-            recv_sem=take_end.at[k],
-            device_id=other,
-            device_id_type=MESH,
-        )
-        for k, other in enumerate(others)
-    ]
-    for copy in copies:
-        copy.start()
-    for copy in copies:
+    zero = jnp.zeros((part, lanes), F32)
+
+    def pass_on(way):
+        pair = pl.ds(2 * way, 2)
+        return [
+            pltpu.make_async_remote_copy(
+                src_ref=moments.at[slab, pair],
+                dst_ref=moments.at[slab, pair],
+                send_sem=send_end.at[way, k],
+                recv_sem=take_end.at[way, k],
+                device_id=other,
+                device_id_type=MESH,
+            )
+            for k, other in enumerate(others)
+        ]
+
+    for way in range(2):
+        for n in (2 * way, 2 * way + 1):
+            moments[slab, n] = encode(ends[n], spare)
+        for copy in pass_on(way):
+            copy.start()
+    for copy in pass_on(0):
         copy.wait()
 
     def carried(direction, n):
@@ -748,15 +758,8 @@
 
     lax.fori_loop(0, rows, forward, carried(1, 0))
 
-    def backward(i, carry):
-        one, two = carry
-        at = rows - 1 - i
-        two = pole * (two + one)
-        one = pole * one
-        filtered[at] += level * one + slope * two
-        return one + freq[at], two
-
-    lax.fori_loop(0, rows, backward, carried(-1, 2))
+    for copy in pass_on(1):
+        copy.wait()
 
     def to_peer(k, g):
         return pltpu.make_async_remote_copy(
@@ -770,10 +773,21 @@
 
     pair = 2
 
-    def unmix(j, _):
+    pairs = groups // pair
+
+    def unmix(turned_j, carry):
+        j = pairs - 1 - turned_j
+        one, two = carry
+        planes = [None] * (pair * count)
+        for i in reversed(range(pair * count)):
+            at_i = j * (pair * count) + i
+            two = pole * (two + one)
+            one = pole * one
+            planes[i] = filtered[at_i] + (level * one + slope * two)
+            one = one + freq[at_i]
         both = []
-        for g in [pair * j + n for n in range(pair)]:
-            blocks = swap_blocks([filtered[g * count + p] for p in range(count)])
+        for n in range(pair):
+            blocks = swap_blocks(planes[n * count : (n + 1) * count])
             top, low = halves(jnp.concatenate(blocks, axis=0))
             both.append(jnp.concatenate([top, top, low], axis=0))
         mixed = matmul(cas_across[...], jnp.concatenate(both, axis=1))
@@ -785,11 +799,12 @@
             for k in range(count - 1):
                 to_peer(k, g).start()
             coming[here, g] = going[here, g]
-        return 0
-
-    lax.fori_loop(0, groups // pair, unmix, 0)
-
-    def back(j, _):
+        return one, two
+
+    lax.fori_loop(0, pairs, unmix, carried(-1, 2))
+
+    def back(turned_j, _):
+        j = pairs - 1 - turned_j
         for g in [pair * j + n for n in range(pair)]:
             for k in range(count - 1):
                 to_peer(k, g).wait()
@@ -800,7 +815,7 @@
                 out[g * count + p] = double[:, :lanes] + double[:, lanes:]
         return 0
 
-    lax.fori_loop(0, groups // pair, back, 0)
+    lax.fori_loop(0, pairs, back, 0)
 
 
 def table(length):
@@ -875,7 +890,7 @@
             pltpu.VMEM((16, padded, depth), F32),
             pltpu.VMEM((2 * observed, depth), BF),
             pltpu.VMEM((4, 8, depth), F32),
-            pltpu.VMEM((slabs, 4, 8, depth), F32),
+            pltpu.VMEM((slabs, 8, depth), F32),
             pltpu.VMEM((2, RING, 2, width, depth), F32),
             pltpu.VMEM((groups, 2, width, depth), F32),
             pltpu.VMEM((RING, width + 16, depth), jnp.int16),
@@ -893,8 +908,9 @@
             pltpu.VMEM((count, groups, part + spare, depth), jnp.int16),
             pltpu.SemaphoreType.DMA,
         ]
-        + [pltpu.SemaphoreType.DMA((slabs - 1,))] * 2
-        + [pltpu.SemaphoreType.DMA((count - 1, groups))] * 2,
+        + [pltpu.SemaphoreType.DMA((2, slabs - 1))] * 2
+        + [pltpu.SemaphoreType.DMA((count - 1, groups))] * 2
+        + [pltpu.VMEM((5, part, depth), F32)],
         compiler_params=pltpu.CompilerParams(
             vmem_limit_bytes=60 * 1024 * 1024, collective_id=1, has_side_effects=True
         ),

time: 81.9 us -> 80.1 us (0.978)
  Pallas kernels: 78.2 us -> 76.5 us
    pallas_call x1, Pallas kernels: 78.2 us -> 76.5 us  [fast(): pl.pallas_call(whole_kernel, out_shape=shape(rows, part, depth), in_specs...]
where the time goes in v5:
time: 80.1 us; the launch traced here: 79.9 us
  Pallas kernels  76.5 us (96%)
  local copies, waits for them, and re-layouts  2.8 us (3%)
    pallas_call x1, Pallas kernels, fast(): pl.pallas_call(whole_kernel, out_shape=shape(rows, part, depth), in_specs...  76.5 us
    unnamed x1, local copies, waits for them, and re-layouts  2.8 us

profile of v5, /device:TPU:0, one launch (start us, length us, event | category | flops | bytes accessed | tf_op | source)
XLA Modules:
  0.0 79.9 jit_solution(7209408159773769637)
XLA Ops:
  0.7 76.5 %whole.1 = f32[48,72,128]{2,1,0:T(8,128)} custom-call(s32[1]{0:T(128)S(6)} %copy.13.well, s32[1,64]{1,0:T(1,128)} %columns.1, f32[64,128]{1,0:T(8,128)} %bitcast.5, bf16[48,288,128]{2,1,0:T(8,128)(2,1)} %logk.1, bf16[48,288,128]{2,1,0:T(8,128)(2,1)} %bitcast.3, bf16[48,288,128]{2,1,0:T(8,128)(2,1)} %bitcast.4, bf16[4,256,256]{2,1,0:T(8,128)(2,1)} %constant.10.clone.turned, ...), custom_call_target="tpu_custom_call" | custom-call | tf_op jit(solution)/shard_map/whole/pallas_call | solution.py:879
  77.1 2.8 %copy.14 = f32[48,72,128]{2,1,0:T(8,128)} copy(f32[48,72,128]{2,1,0:T(8,128)} %whole.1) | data formatting | bytes 3538944

commit v6 on v5

--- a/solution.py
+++ b/solution.py
@@ -278,12 +278,14 @@
     send_back,
     take_back,
     ends,
+    ready,
+    leave_sem,
 ):
     rows, width, depth = logk.shape
     parts = 4
     chunk = rows // parts
-    piece = width // 3
-    pieces = range(3)
+    piece = width // 6
+    pieces = range(6)
     slabs = shared.shape[0]
     slab, here = lax.axis_index("space"), lax.axis_index("test")
     half, core = here // 2, lax.rem(here, 2)
@@ -525,7 +527,31 @@
         for copy in halo(1):
             copy.wait_recv()
 
-    walk(0, 10, (1, 7), (2, 6), (3, 4), (3, 5))
+    def refill(base, n, values):
+        for c in pieces:
+            store(ring, base + n % 4, c, near(soft, n, c) * values[n, at(c), :].astype(F32))
+
+    for n in range(3):
+        prepare(0, whole, n, True)
+    refill(0, 3, wm)
+    residual(0, whole, 1, True)
+    refill(0, 4, wm)
+    residual(0, whole, 2, True)
+    residual(0, whole, 3, True)
+    refill(4, 4, res)
+    for n in (4, 5):
+        for c in pieces:
+            store(ring, 12 + n % 4, c, beside(soft, n - 1, n, n + 1, c, 1.0)[1])
+    sums = [[], [], [], []]
+    image(0, whole, 2, True, None)
+    image(0, whole, 3, True, sums)
+    refill(4, 5, res)
+    image(0, whole, 4, True, sums)
+    refill(8, 5, img)
+    refill(8, 6, img)
+    for n in (3, 4, 5):
+        twice(0, whole, n, sums)
+    keep(sums)
 
     levels_in = pltpu.make_async_copy(heads, lk.at[pl.ds(3, rows)], load_sem.at[0, 0])
     levels_in.start()
@@ -803,6 +829,10 @@
 
     lax.fori_loop(0, pairs, unmix, carried(-1, 2))
 
+    def leave(j):
+        span = pl.ds(j * (pair * count), pair * count)
+        return pltpu.make_async_copy(ready.at[span], out.at[span], leave_sem.at[j])
+
     def back(turned_j, _):
         j = pairs - 1 - turned_j
         for g in [pair * j + n for n in range(pair)]:
@@ -812,10 +842,16 @@
             planes = [decode(coming[t, g], spare) for t in range(count)]
             for p, plane in enumerate(swap_blocks(planes)):
                 double = matmul(jnp.concatenate(halves(plane), axis=1), cas_depth[...])
-                out[g * count + p] = double[:, :lanes] + double[:, lanes:]
+                ready[g * count + p] = double[:, :lanes] + double[:, lanes:]
+        leave(j).start()
         return 0
 
+    def left(j, _):
+        leave(j).wait()
+        return 0
+
     lax.fori_loop(0, pairs, back, 0)
+    lax.fori_loop(0, pairs, left, 0)
 
 
 def table(length):
@@ -880,7 +916,7 @@
         whole_kernel,
         out_shape=shape(rows, part, depth),
         in_specs=[SM, VM, VM, ANY, ANY, ANY, VM, VM, ANY, VM, VM],
-        out_specs=VM,
+        out_specs=ANY,
         scratch_shapes=[pltpu.VMEM((planes, width, depth), BF)] * 2
         + [
             pltpu.VMEM((2, width, depth), BF),
@@ -910,7 +946,11 @@
         ]
         + [pltpu.SemaphoreType.DMA((2, slabs - 1))] * 2
         + [pltpu.SemaphoreType.DMA((count - 1, groups))] * 2
-        + [pltpu.VMEM((5, part, depth), F32)],
+        + [
+            pltpu.VMEM((5, part, depth), F32),
+            pltpu.VMEM((rows, part, depth), F32),
+            pltpu.SemaphoreType.DMA((groups // 2,)),
+        ],
         compiler_params=pltpu.CompilerParams(
             vmem_limit_bytes=60 * 1024 * 1024, collective_id=1, has_side_effects=True
         ),

time: 80.1 us -> 78.2 us (0.976)
  Pallas kernels: 76.5 us -> 74.6 us
    pallas_call x1, Pallas kernels: 76.5 us -> 74.6 us  [fast(): pl.pallas_call(whole_kernel, out_shape=shape(rows, part, depth), in_specs...]
where the time goes in v6:
time: 78.2 us; the launch traced here: 78 us
  Pallas kernels  74.6 us (95%)
  local copies, waits for them, and re-layouts  2.8 us (4%)
    pallas_call x1, Pallas kernels, fast(): pl.pallas_call(whole_kernel, out_shape=shape(rows, part, depth), in_specs...  74.6 us
    unnamed x1, local copies, waits for them, and re-layouts  2.8 us

profile of v6, /device:TPU:0, one launch (start us, length us, event | category | flops | bytes accessed | tf_op | source)
XLA Modules:
  0.0 78.0 jit_solution(589020517814318612)
XLA Ops:
  0.7 74.6 %whole.1 = f32[48,72,128]{2,1,0:T(8,128)} custom-call(s32[1]{0:T(128)S(6)} %copy.13.well, s32[1,64]{1,0:T(1,128)} %columns.1, f32[64,128]{1,0:T(8,128)} %bitcast.5, bf16[48,288,128]{2,1,0:T(8,128)(2,1)} %logk.1, bf16[48,288,128]{2,1,0:T(8,128)(2,1)} %bitcast.3, bf16[48,288,128]{2,1,0:T(8,128)(2,1)} %bitcast.4, bf16[4,256,256]{2,1,0:T(8,128)(2,1)} %constant.10.clone.turned, ...), custom_call_target="tpu_custom_call" | custom-call | tf_op jit(solution)/shard_map/whole/pallas_call | solution.py:915
  75.2 2.8 %copy.14 = f32[48,72,128]{2,1,0:T(8,128)} copy(f32[48,72,128]{2,1,0:T(8,128)} %whole.1) | data formatting | bytes 3538944

commit v7 on v6

--- a/solution.py
+++ b/solution.py
@@ -712,7 +712,7 @@
 
     ends[0:4] = jnp.zeros((4, part, lanes), F32)
     ends[4] = jnp.ones((part, lanes), F32)
-    lag = 4
+    lag = 5
 
     def early(g, _):
         group(g)

time: 78.2 us -> 76.4 us (0.977)
  Pallas kernels: 74.6 us -> 72.8 us
    pallas_call x1, Pallas kernels: 74.6 us -> 72.8 us  [fast(): pl.pallas_call(whole_kernel, out_shape=shape(rows, part, depth), in_specs...]
where the time goes in v7:
time: 76.4 us; the launch traced here: 76.2 us
  Pallas kernels  72.8 us (95%)
  local copies, waits for them, and re-layouts  2.8 us (4%)
    pallas_call x1, Pallas kernels, fast(): pl.pallas_call(whole_kernel, out_shape=shape(rows, part, depth), in_specs...  72.8 us
    unnamed x1, local copies, waits for them, and re-layouts  2.8 us

profile of v7, /device:TPU:0, one launch (start us, length us, event | category | flops | bytes accessed | tf_op | source)
XLA Modules:
  0.0 76.2 jit_solution(5979269548180143485)
XLA Ops:
  0.7 72.8 %whole.1 = f32[48,72,128]{2,1,0:T(8,128)} custom-call(s32[1]{0:T(128)S(6)} %copy.13.well, s32[1,64]{1,0:T(1,128)} %columns.1, f32[64,128]{1,0:T(8,128)} %bitcast.5, bf16[48,288,128]{2,1,0:T(8,128)(2,1)} %logk.1, bf16[48,288,128]{2,1,0:T(8,128)(2,1)} %bitcast.3, bf16[48,288,128]{2,1,0:T(8,128)(2,1)} %bitcast.4, bf16[4,256,256]{2,1,0:T(8,128)(2,1)} %constant.10.clone.turned, ...), custom_call_target="tpu_custom_call" | custom-call | tf_op jit(solution)/shard_map/whole/pallas_call | solution.py:915
  73.4 2.8 %copy.14 = f32[48,72,128]{2,1,0:T(8,128)} copy(f32[48,72,128]{2,1,0:T(8,128)} %whole.1) | data formatting | bytes 3538944
